TPU v7x, 32 devices: a whole 2x2x4 slice. The times are simulated.
32 devices in a mesh: roll: 16 (over z, y, core), rep: 2 (over x).
Axes of the slice: x: 2, y: 2, z: 4, core: 2. Of those that a mesh axis runs over, the one named last changes fastest.
Arguments:
- rollout: bfloat16 [65536, 256], P(('roll', 'rep')), may hold values from -7.8 to 7.8
- demo: bfloat16 [32768, 256], P('roll'), may hold values from -6 to 6
- projection: bfloat16 [256, 256], replicated, may hold values from -0.375 to 0.375
- location: int32 [256], replicated, may hold values from 0 to 255, as said below
- pair_block: int32 [512, 8], P(('roll', 'rep')), may hold values from 0 to 255, as said below
- pair_count: int32 [512], P(('roll', 'rep')), may hold values from 1 to 8, as said below
Outputs:
- reward: float32 [65536], P(('roll', 'rep'))
- rollout_potential: float32 [65536], P(('roll', 'rep'))
- demo_potential: float32 [32768], P('roll')
Inputs may be any that keep to these rules, and one draw needn't show every extreme that they name: location is a permutation; demonstration block d is stored block location[d], held by roll index location[d] // 16. `pair_block`: among the slots in use of the 16 rollout blocks of one device, at most 8 name blocks stored on any one roll index, and some device reaches 8. `pair_count`: on one roll index every rollout block uses all 8 slots.
All inputs are finite; a program needn't handle non-finite values.
Results may differ from a plain program's by a relative error of at most 0.0024.
Values may be sent and summed in bfloat16 or wider, within the bound.
A program may use at most 128 MiB of HBM per device.

v0:
```python
import jax
import jax.numpy as jnp
from jax import lax
from jax.sharding import PartitionSpec as P

ITERS = 2


EPSILON = 0.02
UNMATCHED = 2.0
SLACK = -100.0
NEGLIGIBLE = -1e30


def joined(value, axis, join):
    pieces = jax.tree.map(lambda part: lax.all_gather(part, axis), value)
    head = jax.tree.map(lambda part: part[0], pieces)
    tail = jax.tree.map(lambda part: part[1:], pieces)
    subtotal, _ = lax.scan(lambda subtotal, share: (join(subtotal, share), None), head, tail)
    return subtotal


def tile_costs(left_codes, right_codes):
    crossed = jnp.einsum(
        "pie,pje->pij", left_codes, right_codes, preferred_element_type=jnp.float32
    )
    norm_left = jnp.einsum(
        "pie,pie->pi", left_codes, left_codes, preferred_element_type=jnp.float32
    )
    norm_right = jnp.einsum(
        "pje,pje->pj", right_codes, right_codes, preferred_element_type=jnp.float32
    )
    return (norm_left[:, :, None] + norm_right[:, None, :] - 2.0 * crossed) / left_codes.shape[2]


def row_part(costs, demo_pot, final):
    scores = (demo_pot[:, None, :] - costs) / EPSILON
    largest = jnp.max(scores, axis=2)
    shifted = jnp.exp(scores - largest[:, :, None])
    summed = jnp.sum(shifted, axis=2)
    row_lse = largest + jnp.log(summed)
    if final:
        return (row_lse, jnp.sum(shifted * costs, axis=2) / summed)
    return (row_lse, None)


def column_part(costs, roll_pot):
    scores = (roll_pot[:, :, None] - costs) / EPSILON
    largest = jnp.max(scores, axis=1)
    return largest + jnp.log(jnp.sum(jnp.exp(scores - largest[:, None, :]), axis=1))


def combine(earlier, later):
    largest = jnp.maximum(earlier[0], later[0])
    return (
        largest,
        earlier[1] * jnp.exp(earlier[0] - largest) + later[1] * jnp.exp(later[0] - largest),
    )


def demo_side(column_lse, wanted, demo_count):
    belongs = (wanted[:, None] == jnp.arange(demo_count, dtype=jnp.int32)[None, :])[:, :, None]
    largest = jnp.max(jnp.where(belongs, column_lse[:, None, :], NEGLIGIBLE), axis=0)
    summed = jnp.sum(
        jnp.where(belongs, jnp.exp(column_lse[:, None, :] - largest[None]), 0.0), axis=0
    )
    largest, summed = joined((largest, summed), "rep", combine)
    highest = jnp.maximum(largest, SLACK)
    log_total = highest + jnp.log(summed * jnp.exp(largest - highest) + jnp.exp(SLACK - highest))
    return -EPSILON * log_total


def rollout_side(row_lse, weighted, home_block, roll_blocks):
    belongs = (home_block[:, None] == jnp.arange(roll_blocks, dtype=jnp.int32)[None, :])[:, :, None]
    spread_out = jnp.where(belongs, row_lse[:, None, :], NEGLIGIBLE)
    largest = jnp.maximum(jnp.max(spread_out, axis=0), SLACK)
    summed = jnp.sum(
        jnp.where(belongs, jnp.exp(row_lse[:, None, :] - largest[None]), 0.0), axis=0
    ) + jnp.exp(SLACK - largest)
    log_total = largest + jnp.log(summed)
    potential = -EPSILON * log_total
    if weighted is None:
        return (potential, None)
    shares = jnp.where(
        belongs, jnp.exp(row_lse[:, None, :] - log_total[None]) * weighted[:, None, :], 0.0
    )
    reward = -(jnp.sum(shares, axis=0) + jnp.exp(SLACK - log_total) * UNMATCHED)
    return (potential, reward)


def body(rollout, demo, projection, location, pair_block, pair_count):
    roll_blocks, pair_slots = pair_block.shape
    block_len = rollout.shape[0] // roll_blocks
    features = projection.shape[1]
    demo_count = demo.shape[0] // block_len
    owners_n = lax.axis_size("roll")
    slot_count = roll_blocks * pair_slots
    capacity = max(1, slot_count // owners_n)
    positions = owners_n * capacity
    roll_codes = jnp.dot(rollout, projection, preferred_element_type=jnp.float32).astype(
        jnp.bfloat16
    )
    demo_codes = jnp.dot(demo, projection, preferred_element_type=jnp.float32).astype(jnp.bfloat16)
    roll_tiles = roll_codes.reshape(roll_blocks, block_len, features)
    demo_tiles = demo_codes.reshape(demo_count, block_len, features)
    chosen = pair_block.reshape(slot_count)
    active = (jnp.arange(pair_slots, dtype=jnp.int32)[None, :] < pair_count[:, None]).reshape(
        slot_count
    )
    stored = location[chosen]
    owner_roll = stored // demo_count
    local_block = stored % demo_count
    slot_ids = jnp.arange(slot_count, dtype=jnp.int32)
    earlier = (
        (owner_roll[:, None] == owner_roll[None, :])
        & active[None, :]
        & (slot_ids[None, :] < slot_ids[:, None])
    )
    position_rank = jnp.sum(earlier.astype(jnp.int32), axis=1)
    slot_place = jnp.where(active, owner_roll * capacity + position_rank, positions)
    requested = jnp.full((positions,), -1, jnp.int32).at[slot_place].set(local_block, mode="drop")
    home_block = (
        jnp.full((positions,), -1, jnp.int32)
        .at[slot_place]
        .set(slot_ids // pair_slots, mode="drop")
    )
    wanted = lax.all_to_all(
        requested.reshape(owners_n, capacity), "roll", split_axis=0, concat_axis=0, tiled=True
    ).reshape(positions)
    serve_index = jnp.maximum(wanted, 0)
    home_index = jnp.maximum(home_block, 0)
    roll_pot = jnp.zeros((roll_blocks, block_len), jnp.float32)
    demo_pot = jnp.zeros((demo_count, block_len), jnp.float32)
    reward = jnp.zeros((roll_blocks, block_len), jnp.float32)
    outgoing = demo_tiles[serve_index]
    arrived = lax.all_to_all(
        outgoing.reshape(owners_n, capacity, block_len, features),
        "roll",
        split_axis=0,
        concat_axis=0,
        tiled=True,
    )
    left_codes = roll_tiles[home_index]
    right_codes = arrived.reshape(positions, block_len, features)
    stored_costs = tile_costs(left_codes, right_codes)
    for iteration in range(ITERS):
        costs = stored_costs
        column_lse = column_part(costs, roll_pot[home_index])
        returned = lax.all_to_all(
            column_lse.reshape(owners_n, capacity, block_len),
            "roll",
            split_axis=0,
            concat_axis=0,
            tiled=True,
        )
        demo_pot = demo_side(returned.reshape(positions, block_len), wanted, demo_count)
        pot_sent = lax.all_to_all(
            demo_pot[serve_index].reshape(owners_n, capacity, block_len),
            "roll",
            split_axis=0,
            concat_axis=0,
            tiled=True,
        )
        costs = stored_costs
        final = iteration == ITERS - 1
        row_lse, weighted = row_part(costs, pot_sent.reshape(positions, block_len), final)
        roll_pot, row_reward = rollout_side(row_lse, weighted, home_block, roll_blocks)
        if final:
            reward = row_reward
    return (reward.reshape(-1), roll_pot.reshape(-1), demo_pot.reshape(-1))


def solution(mesh):
    placed = (
        P(("roll", "rep"), None),
        P("roll", None),
        P(),
        P(),
        P(("roll", "rep"), None),
        P(("roll", "rep")),
    )
    return jax.shard_map(
        body,
        mesh=mesh,
        in_specs=placed,
        out_specs=(P(("roll", "rep")), P(("roll", "rep")), P("roll")),
        check_vma=False,
    )
```

profile of v0, /device:TPU:0, one launch (start us, length us, event | category | flops | bytes accessed | tf_op | source)
XLA Modules:
  0.0 339.9 jit_solution(15542942055266112973)
XLA Ops:
  2.5 1.6 gather_fusion
  4.4 1.0 scatter_custom_fusion.1
  6.1 7.4 %all-to-all-start = ((s32[16,1,8]{2,1,0:T(1,128)}), s32[16,1,8]{2,1,0:T(1,128)S(1)}, u32[]{:S(2)}, u32[]{:S(2)}) async-start(s32[16,1,8]{2,1,0:T(1,128)} %bitcast.4), calls=%async_computation | async-start | bytes 16384 | tf_op jit(solution)/shard_map/all_to_all | solution.py:127
  13.5 1.3 convolution_convert_fusion
  14.8 5.0 %all-to-all-done = s32[16,1,8]{2,1,0:T(1,128)S(1)} async-done(((s32[16,1,8]{2,1,0:T(1,128)}), s32[16,1,8]{2,1,0:T(1,128)S(1)}, u32[]{:S(2)}, u32[]{:S(2)}) %all-to-all-start) | async-done | bytes 544 | tf_op jit(solution)/shard_map/all_to_all | solution.py:127
  21.1 6.4 %gather_fusion.3 = bf16[128,128,256]{2,1,0:T(8,128)(2,1)} fusion(bf16[16,128,256]{2,1,0:T(8,128)(2,1)S(1)} %bitcast.94, s32[1024]{0:T(1024)S(1)} %pad_clamp_fusion), kind=kCustom, calls=%fused_computation.3 | custom fusion | bytes 16777728 | tf_op jit(solution)/shard_map/gather | solution.py:135
  27.5 4.9 %all-to-all-start.1 = ((bf16[16,8,128,256]{3,2,1,0:T(8,128)(2,1)}), bf16[16,8,128,256]{3,2,1,0:T(8,128)(2,1)}, u32[]{:S(2)}, u32[]{:S(2)}) async-start(bf16[16,8,128,256]{3,2,1,0:T(8,128)(2,1)} %bitcast.96), calls=%async_computation.1 | async-start | bytes 16777216 | tf_op jit(solution)/shard_map/all_to_all | solution.py:136
  32.4 1.2 scatter_custom_fusion
  34.1 6.4 %gather_fusion.2 = bf16[128,128,256]{2,1,0:T(8,128)(2,1)} fusion(bf16[16,128,256]{2,1,0:T(8,128)(2,1)S(1)} %bitcast.95, s32[1024]{0:T(1024)S(1)} %pad_clamp_fusion.1), kind=kCustom, calls=%fused_computation.2 | custom fusion | bytes 16777728 | tf_op jit(solution)/shard_map/gather | solution.py:143
  41.1 5.6 %fusion.1 = f32[128,128]{1,0:T(8,128)S(1)} fusion(bf16[128,128,256]{2,1,0:T(8,128)(2,1)} %gather_fusion.2), kind=kLoop, calls=%fused_computation.12 | loop fusion | flops 12566528 | bytes 8454144 | tf_op jit(solution)/shard_map/pie,pie->pi/dot_general | solution.py:27
  46.8 136.3 %all-to-all-done.1 = bf16[16,8,128,256]{3,2,1,0:T(8,128)(2,1)} async-done(((bf16[16,8,128,256]{3,2,1,0:T(8,128)(2,1)}), bf16[16,8,128,256]{3,2,1,0:T(8,128)(2,1)}, u32[]{:S(2)}, u32[]{:S(2)}) %all-to-all-start.1) | async-done | bytes 8388640 | tf_op jit(solution)/shard_map/all_to_all | solution.py:136
  183.1 5.6 %fusion = f32[128,128]{1,0:T(8,128)S(1)} fusion(bf16[16,8,128,256]{3,2,1,0:T(8,128)(2,1)} %all-to-all-done.1), kind=kLoop, calls=%fused_computation.10 | loop fusion | flops 12566528 | bytes 8454144 | tf_op jit(solution)/shard_map/pje,pje->pj/dot_general | solution.py:30
  188.7 8.9 %fusion.2 = (f32[128,128]{1,0:T(8,128)S(1)}, f32[128,128,128]{1,2,0:T(8,128)S(1)}) fusion(f32[128,128]{1,0:T(8,128)S(1)} %gather_fusion.1, bf16[128,128,256]{2,1,0:T(8,128)(2,1)} %gather_fusion.2, bf16[128,128,256]{2,1,0:T(8,128)(2,1)} %bitcast.8, f32[128,128]{1,0:T(8,128)S(1)} %fusion, f32[128,128]{1,0:T(8,128)S(1)} %fusion.1), kind=kOutput, calls=%fused_computation.23 | convolution fusion | flops 1088405504 | bytes 25427968 | tf_op jit(solution)/shard_map/pie,pje->pij/dot_general | solution.py:24
  197.6 3.2 copy-done.1
  200.8 4.8 %exponential_reduce_fusion.2 = f32[128,128]{1,0:T(8,128)S(1)} fusion(f32[128,128,128]{1,2,0:T(8,128)S(1)} %get-tuple-element.44, f32[128,128]{1,0:T(8,128)S(1)} %get-tuple-element.43, f32[128,128]{1,0:T(8,128)S(1)} %gather_fusion.1), kind=kLoop, calls=%fused_computation.20 | loop fusion | flops 8372224 | bytes 8585216 | tf_op jit(solution)/shard_map/reduce_sum | solution.py:50
  206.2 36.5 %all-to-all-start.2 = ((f32[16,8,128]{2,1,0:T(8,128)}), f32[16,8,128]{2,1,0:T(8,128)S(1)}, u32[]{:S(2)}, u32[]{:S(2)}) async-start(f32[16,8,128]{2,1,0:T(8,128)} %add_bitcast_fusion.1), calls=%async_computation.2 | async-start | bytes 131072 | tf_op jit(solution)/shard_map/all_to_all | solution.py:149
  242.8 6.8 %all-to-all-done.2 = f32[16,8,128]{2,1,0:T(8,128)S(1)} async-done(((f32[16,8,128]{2,1,0:T(8,128)}), f32[16,8,128]{2,1,0:T(8,128)S(1)}, u32[]{:S(2)}, u32[]{:S(2)}) %all-to-all-start.2) | async-done | bytes 65568 | tf_op jit(solution)/shard_map/all_to_all | solution.py:149
  250.4 4.4 %all-gather = f32[32,128]{1,0:T(8,128)S(1)} all-gather(f32[16,128]{1,0:T(8,128)S(1)} %select_reduce_fusion.8), channel_id=2, replica_groups=mesh['roll'=16,'rep'=2] {'rep'}, dimensions={0}, use_global_device_ids=true | all-gather | bytes 24576 | tf_op jit(solution)/shard_map/all_gather | solution.py:16
  254.7 4.4 %all-gather.1 = f32[32,128]{1,0:T(8,128)S(1)} all-gather(f32[16,128]{1,0:T(8,128)S(1)} %select_reduce_fusion.7), channel_id=3, replica_groups=mesh['roll'=16,'rep'=2] {'rep'}, dimensions={0}, use_global_device_ids=true | all-gather | bytes 24576 | tf_op jit(solution)/shard_map/all_gather | solution.py:16
  259.1 1.2 gather_fusion.4
  260.4 3.7 %all-to-all-start.3 = ((f32[16,8,128]{2,1,0:T(8,128)}), f32[16,8,128]{2,1,0:T(8,128)S(1)}, u32[]{:S(2)}, u32[]{:S(2)}) async-start(f32[16,8,128]{2,1,0:T(8,128)} %bitcast.11), calls=%async_computation.3 | async-start | bytes 131072 | tf_op jit(solution)/shard_map/all_to_all | solution.py:157
  264.2 6.5 %all-to-all-done.3 = f32[16,8,128]{2,1,0:T(8,128)S(1)} async-done(((f32[16,8,128]{2,1,0:T(8,128)}), f32[16,8,128]{2,1,0:T(8,128)S(1)}, u32[]{:S(2)}, u32[]{:S(2)}) %all-to-all-start.3) | async-done | bytes 65568 | tf_op jit(solution)/shard_map/all_to_all | solution.py:157
  270.7 5.7 %fusion.3 = f32[128,128]{1,0:T(8,128)S(1)} fusion(f32[128,128,128]{1,2,0:T(8,128)} %copy-done.1, f32[128,128]{1,0:T(8,128)S(1)} %bitcast.97), kind=kLoop, calls=%fused_computation.24 | loop fusion | flops 6275072 | bytes 8519680 | tf_op jit(solution)/shard_map/reduce_max | solution.py:38
  276.6 4.9 %exponential_reduce_fusion.1 = f32[128,128]{1,0:T(8,128)S(1)} fusion(f32[128,128,128]{1,2,0:T(8,128)S(1)} %copy-done.2, f32[128,128]{1,0:T(8,128)S(1)} %fusion.3, f32[128,128]{1,0:T(8,128)S(1)} %bitcast.98), kind=kLoop, calls=%fused_computation.18 | loop fusion | flops 8372224 | bytes 8585216 | tf_op jit(solution)/shard_map/reduce_sum | solution.py:40
  283.0 5.6 %fusion.4 = f32[128,128]{1,0:T(8,128)S(1)} fusion(f32[128,128,128]{1,2,0:T(8,128)} %copy-done.1, f32[128,128]{1,0:T(8,128)S(1)} %gather_fusion.5), kind=kLoop, calls=%fused_computation.25 | loop fusion | flops 6275072 | bytes 8519680 | tf_op jit(solution)/shard_map/reduce_max | solution.py:49
  288.7 6.9 %exponential_reduce_fusion = f32[128,128]{1,0:T(8,128)S(1)} fusion(f32[128,128,128]{1,2,0:T(8,128)} %copy-done.1, f32[128,128]{1,0:T(8,128)S(1)} %fusion.4, f32[128,128]{1,0:T(8,128)S(1)} %gather_fusion.5), kind=kLoop, calls=%fused_computation.16 | loop fusion | flops 8372224 | bytes 8585216 | tf_op jit(solution)/shard_map/reduce_sum | solution.py:50
  295.6 9.5 %all_to_all.34 = f32[16,8,128]{2,1,0:T(8,128)S(1)} all-to-all(f32[16,8,128]{2,1,0:T(8,128)S(1)} %add_bitcast_fusion), channel_id=1, replica_groups=mesh['roll'=16,'rep'=2] {'roll'}, dimensions={0} | all-to-all | bytes 131072 | tf_op jit(solution)/shard_map/all_to_all | solution.py:149
  305.9 4.4 %all-gather.2 = f32[32,128]{1,0:T(8,128)S(1)} all-gather(f32[16,128]{1,0:T(8,128)S(1)} %select_reduce_fusion.4), channel_id=4, replica_groups=mesh['roll'=16,'rep'=2] {'rep'}, dimensions={0}, use_global_device_ids=true | all-gather | bytes 24576 | tf_op jit(solution)/shard_map/all_gather | solution.py:16
  310.3 4.4 %all-gather.3 = f32[32,128]{1,0:T(8,128)S(1)} all-gather(f32[16,128]{1,0:T(8,128)S(1)} %select_reduce_fusion.3), channel_id=5, replica_groups=mesh['roll'=16,'rep'=2] {'rep'}, dimensions={0}, use_global_device_ids=true | all-gather | bytes 24576 | tf_op jit(solution)/shard_map/all_gather | solution.py:16
  315.3 9.5 %all_to_all.35 = f32[16,8,128]{2,1,0:T(8,128)S(1)} all-to-all(f32[16,8,128]{2,1,0:T(8,128)S(1)} %bitcast.105), channel_id=1, replica_groups=mesh['roll'=16,'rep'=2] {'roll'}, dimensions={0} | all-to-all | bytes 131072 | tf_op jit(solution)/shard_map/all_to_all | solution.py:157
  324.8 5.2 %fusion.5 = f32[128,128]{1,0:T(8,128)S(1)} fusion(f32[128,128,128]{1,2,0:T(8,128)} %copy-done.1, f32[128,128]{1,0:T(8,128)S(1)} %bitcast.99), kind=kLoop, calls=%fused_computation.26 | loop fusion | flops 6275072 | bytes 8519680 | tf_op jit(solution)/shard_map/reduce_max | solution.py:38
  330.0 7.9 %fusion.6 = (f32[128,128]{1,0:T(8,128)S(1)}, f32[128,128]{1,0:T(8,128)S(1)}) fusion(f32[128,128,128]{1,2,0:T(8,128)} %copy-done.1, f32[128,128]{1,0:T(8,128)S(1)} %fusion.5, f32[128,128]{1,0:T(8,128)S(1)} %bitcast.100), kind=kLoop, calls=%fused_computation.27 | loop fusion | flops 12550144 | bytes 8650752 | tf_op jit(solution)/shard_map/reduce_sum | solution.py:40
  (55 shorter events, 11.9 us)
Async XLA Ops:
  0.6 12.8 %copy-start = (bf16[2048,256]{1,0:T(8,128)(2,1)S(1)}, bf16[2048,256]{1,0:T(8,128)(2,1)}, u32[]{:S(2)}) copy-start(bf16[2048,256]{1,0:T(8,128)(2,1)} %param.7) | copy-start | bytes 3145732
  6.1 13.7 %all-to-all-start = ((s32[16,1,8]{2,1,0:T(1,128)}), s32[16,1,8]{2,1,0:T(1,128)S(1)}, u32[]{:S(2)}, u32[]{:S(2)}) async-start(s32[16,1,8]{2,1,0:T(1,128)} %bitcast.4), calls=%async_computation | async-start | bytes 16384 | tf_op jit(solution)/shard_map/all_to_all | solution.py:127
  27.5 6.1 %copy-start.3 = (bf16[2048,256]{1,0:T(8,128)(2,1)S(1)}, bf16[2048,256]{1,0:T(8,128)(2,1)}, u32[]{:S(2)}) copy-start(bf16[2048,256]{1,0:T(8,128)(2,1)} %param.6) | copy-start | bytes 3145732
  27.5 6.1 %copy-start.4 = (bf16[256,256]{1,0:T(8,128)(2,1)S(1)}, bf16[256,256]{1,0:T(8,128)(2,1)}, u32[]{:S(2)}) copy-start(bf16[256,256]{1,0:T(8,128)(2,1)} %param.8) | copy-start | bytes 393220
  27.5 155.5 %all-to-all-start.1 = ((bf16[16,8,128,256]{3,2,1,0:T(8,128)(2,1)}), bf16[16,8,128,256]{3,2,1,0:T(8,128)(2,1)}, u32[]{:S(2)}, u32[]{:S(2)}) async-start(bf16[16,8,128,256]{3,2,1,0:T(8,128)(2,1)} %bitcast.96), calls=%async_computation.1 | async-start | bytes 16777216 | tf_op jit(solution)/shard_map/all_to_all | solution.py:136
  197.6 3.2 copy-start.1
  206.2 43.4 %all-to-all-start.2 = ((f32[16,8,128]{2,1,0:T(8,128)}), f32[16,8,128]{2,1,0:T(8,128)S(1)}, u32[]{:S(2)}, u32[]{:S(2)}) async-start(f32[16,8,128]{2,1,0:T(8,128)} %add_bitcast_fusion.1), calls=%async_computation.2 | async-start | bytes 131072 | tf_op jit(solution)/shard_map/all_to_all | solution.py:149
  260.4 10.4 %all-to-all-start.3 = ((f32[16,8,128]{2,1,0:T(8,128)}), f32[16,8,128]{2,1,0:T(8,128)S(1)}, u32[]{:S(2)}, u32[]{:S(2)}) async-start(f32[16,8,128]{2,1,0:T(8,128)} %bitcast.11), calls=%async_computation.3 | async-start | bytes 131072 | tf_op jit(solution)/shard_map/all_to_all | solution.py:157
  270.7 5.9 %copy-start.2 = (f32[128,128,128]{1,2,0:T(8,128)S(1)}, f32[128,128,128]{1,2,0:T(8,128)}, u32[]{:S(2)}) copy-start(f32[128,128,128]{1,2,0:T(8,128)} %copy-done.1) | copy-start | bytes 25165828
where the time goes:
time: 341 us; the launch traced here: 340 us
  waiting for transfers between devices  155 us (45%)
  other arithmetic  59.1 us (17%)
  starting transfers between devices  52.4 us (15%)
  blocking collectives  36.4 us (11%)
  local copies, waits for them, and re-layouts  25.6 us (8%)
  matrix products  10.6 us (3%)
    all_to_all x1, waiting for transfers between devices, body(): lax.all_to_all(outgoing.reshape(owners_n, capacity, block_len, features),...  136 us
    all_to_all x1, starting transfers between devices, body(): lax.all_to_all(column_lse.reshape(owners_n, capacity, block_len), 'roll',...  36.5 us
    all_gather x4, blocking collectives, joined(): pieces = jax.tree.map(lambda part: lax.all_gather(part, axis), value)  17.4 us
    reduce_sum x2, other arithmetic, row_part(): summed = jnp.sum(shifted, axis=2)  12.8 us
    reduce_sum x2, other arithmetic, column_part(): jnp.sum(jnp.exp(scores - largest[:, None, :]), axis=1)  11.7 us
    reduce_max x2, other arithmetic, row_part(): largest = jnp.max(scores, axis=2)  10.9 us
    all_to_all x1, blocking collectives, body(): lax.all_to_all(column_lse.reshape(owners_n, capacity, block_len), 'roll',...  9.48 us
    all_to_all x1, blocking collectives, body(): lax.all_to_all(demo_pot[serve_index].reshape(owners_n, capacity, block_le...  9.47 us
  transfers between devices with their start and end apart: 4, of which 4 were waited for; matrix products, arithmetic and copies ran while one was open for 5% of the time, Pallas kernels for 0%

commit v1 on v0

v1 whole, which is shorter than its diff:
```python
import functools
import math

import jax
import jax.numpy as jnp
from jax import lax
from jax.experimental import pallas as pl
from jax.experimental.pallas import tpu as pltpu
from jax.sharding import PartitionSpec as P

EPSILON = 0.02
UNMATCHED = 2.0
SLACK = -100.0
LOG2E = math.log2(math.e)
SCALE = LOG2E / EPSILON
SHIFT = 50.0 * LOG2E
FLOOR = math.exp(SLACK + 50.0)
UNROLL = 4


def pass_kernel(kind, total_ref, home_ref, target_ref, u_ref, v_ref, unorm_ref, vnorm_ref, pot_ref, *rest):
    roll_blocks, blk = unorm_ref.shape
    feats = u_ref.shape[1]
    unit = SCALE / feats
    if kind == "column":
        out_ref, row_term, col_acc = rest
        col_acc[...] = jnp.zeros_like(col_acc)
    elif kind == "row":
        out_ref, row_term, col_term, acc = rest
        acc[...] = jnp.zeros_like(acc)
    else:
        out_ref, row_term, col_term, acc, wacc = rest
        acc[...] = jnp.zeros_like(acc)
        wacc[...] = jnp.zeros_like(wacc)

    def prepare(b, carry):
        line = unorm_ref[pl.ds(b, 1), :] * (-unit)
        if kind == "column":
            line = line + (pot_ref[pl.ds(b, 1), :] + SHIFT)
        row_term[pl.ds(b * blk, blk), :] = jnp.transpose(jnp.broadcast_to(line, (blk, blk)))
        return carry

    lax.fori_loop(0, roll_blocks, prepare, 0)
    if kind != "column":
        col_term[...] = pot_ref[...] + SHIFT

    total = total_ref[0]

    def step(k, carry):
        parts = []
        for p in range(UNROLL):
            at = k * UNROLL + p
            b = home_ref[at]
            t = target_ref[at]
            live = jnp.where(at < total, 0.0, -1e30)
            rows = pl.ds(pl.multiple_of(b * blk, blk), blk)
            crossed = lax.dot_general(
                u_ref[rows, :],
                v_ref[pl.ds(pl.multiple_of(t * blk, blk), blk), :],
                (((1,), (1,)), ((), ())),
                preferred_element_type=jnp.float32,
            )
            y = crossed * (2.0 * unit) + row_term[rows, :]
            line = vnorm_ref[pl.ds(t, 1), :] * (-unit)
            if kind == "column":
                e = jnp.exp2(y + (line + live))
                parts.append((t, jnp.sum(e.reshape(blk // 8, 8, blk), axis=0)))
            elif kind == "row":
                e = jnp.exp2(y + (line + (col_term[pl.ds(t, 1), :] + live)))
                parts.append((rows, e))
            else:
                y = y + line
                e = jnp.exp2(y + (col_term[pl.ds(t, 1), :] + live))
                parts.append((rows, e, e * y))
        for part in parts:
            if kind == "column":
                at8 = pl.ds(pl.multiple_of(part[0] * 8, 8), 8)
                col_acc[at8, :] = col_acc[at8, :] + part[1]
            else:
                acc[part[0], :] = acc[part[0], :] + part[1]
                if kind == "final":
                    wacc[part[0], :] = wacc[part[0], :] + part[2]
        return carry

    lax.fori_loop(0, (total + UNROLL - 1) // UNROLL, step, 0)

    if kind == "column":
        targets = out_ref.shape[0]
        out_ref[...] = jnp.sum(col_acc[...].reshape(targets, 8, blk), axis=1)
    else:

        def finish(b, carry):
            rows = pl.ds(pl.multiple_of(b * blk, blk), blk)
            out_ref[0, pl.ds(b, 1), :] = jnp.sum(jnp.transpose(acc[rows, :]), axis=0, keepdims=True)
            if kind == "final":
                out_ref[1, pl.ds(b, 1), :] = jnp.sum(
                    jnp.transpose(wacc[rows, :]), axis=0, keepdims=True
                ) * (-1.0 / SCALE)
            return carry

        lax.fori_loop(0, roll_blocks, finish, 0)


def run_pass(kind, lists, u, v, unorm, vnorm, pot):
    roll_blocks, blk = unorm.shape
    targets = vnorm.shape[0]
    smem = pl.BlockSpec(memory_space=pltpu.SMEM)
    vmem = pl.BlockSpec(memory_space=pltpu.VMEM)
    frames = pltpu.VMEM((roll_blocks * blk, blk), jnp.float32)
    if kind == "column":
        out = jax.ShapeDtypeStruct((targets, blk), jnp.float32)
        scratch = [frames, pltpu.VMEM((targets * 8, blk), jnp.float32)]
    else:
        out = jax.ShapeDtypeStruct((2 if kind == "final" else 1, roll_blocks, blk), jnp.float32)
        scratch = [frames, pltpu.VMEM((targets, blk), jnp.float32), frames]
        if kind == "final":
            scratch.append(frames)
    pairs = lists[1].shape[0] // 2
    return pl.pallas_call(
        functools.partial(pass_kernel, kind),
        out_shape=out,
        in_specs=[smem] * 3 + [vmem] * 5,
        out_specs=vmem,
        scratch_shapes=scratch,
        compiler_params=pltpu.CompilerParams(vmem_limit_bytes=56 * 1024 * 1024),
        cost_estimate=pl.CostEstimate(
            flops=2 * pairs * blk * blk * u.shape[1],
            bytes_accessed=2 * (u.size + v.size),
            transcendentals=pairs * blk * blk,
        ),
        name="pass_" + kind,
    )(*lists, u, v, unorm, vnorm, pot)


def listed(pair_block, pair_count, location, demo_count, share, part):
    roll_blocks, slots = pair_block.shape
    n = roll_blocks * slots
    names = jnp.arange(location.shape[0], dtype=jnp.int32)
    flat = pair_block.reshape(n)
    stored = jnp.sum(jnp.where(flat[:, None] == names[None, :], location[None, :], 0), axis=1)
    active = (jnp.arange(slots, dtype=jnp.int32)[None, :] < pair_count[:, None]).reshape(n)
    local = stored % demo_count
    mine = active & (local // share == part)
    target = (stored // demo_count) * share + local % share
    ids = jnp.arange(n, dtype=jnp.int32)
    rank = jnp.sum((mine[None, :] & (ids[None, :] < ids[:, None])).astype(jnp.int32), axis=1)
    place = jnp.where(mine, rank, -1)
    hit = place[None, :] == ids[:, None]
    home = jnp.sum(jnp.where(hit, (ids // slots)[None, :], 0), axis=1)
    target = jnp.sum(jnp.where(hit, target[None, :], 0), axis=1)
    total = jnp.sum(mine.astype(jnp.int32)).reshape(1)
    return total, jnp.pad(home, (0, UNROLL)), jnp.pad(target, (0, UNROLL))


def project(frames, projection):
    return jnp.dot(frames, projection, preferred_element_type=jnp.float32).astype(jnp.bfloat16)


def norms(codes, blk):
    wide = codes.astype(jnp.float32)
    return jnp.sum(wide * wide, axis=1).reshape(-1, blk)


def body(rollout, demo, projection, location, pair_block, pair_count):
    own_blocks = pair_block.shape[0]
    blk = rollout.shape[0] // own_blocks
    demo_count = demo.shape[0] // blk
    reps = lax.axis_size("rep")
    part = lax.axis_index("rep")
    share = demo_count // reps
    lists = listed(
        lax.all_gather(pair_block, "rep", tiled=True),
        lax.all_gather(pair_count, "rep", tiled=True),
        location,
        demo_count,
        share,
        part,
    )
    own_demo = lax.dynamic_slice_in_dim(demo, part * (share * blk), share * blk, 0)
    own_v = project(own_demo, projection)
    own_u = project(rollout, projection)
    v = lax.all_gather(own_v, "roll", tiled=True)
    vnorm = lax.all_gather(norms(own_v, blk), "roll", tiled=True)
    u = lax.all_gather(own_u, "rep", tiled=True)
    unorm = lax.all_gather(norms(own_u, blk), "rep", tiled=True)

    roll_pot = jnp.zeros_like(unorm)
    for iteration in range(2):
        sums = run_pass("column", lists, u, v, unorm, vnorm, roll_pot)
        demo_pot = SHIFT - jnp.log2(lax.psum(sums, "roll") + FLOOR)
        kind = "final" if iteration == 1 else "row"
        sums = run_pass(kind, lists, u, v, unorm, vnorm, demo_pot)
        sums = lax.psum(sums, "rep")
        heights = sums[0] + FLOOR
        roll_pot = SHIFT - jnp.log2(heights)
    reward = -(sums[1] + UNMATCHED * FLOOR) / heights
    mine = lax.axis_index("roll") * share
    own_pot = lax.all_gather(lax.dynamic_slice_in_dim(demo_pot, mine, share, 0), "rep", tiled=True)
    first = part * own_blocks
    return (
        lax.dynamic_slice_in_dim(reward, first, own_blocks, 0).reshape(-1),
        lax.dynamic_slice_in_dim(roll_pot, first, own_blocks, 0).reshape(-1) / SCALE,
        own_pot.reshape(-1) / SCALE,
    )


def solution(mesh):
    placed = (
        P(("roll", "rep"), None),
        P("roll", None),
        P(),
        P(),
        P(("roll", "rep"), None),
        P(("roll", "rep")),
    )
    return jax.shard_map(
        body,
        mesh=mesh,
        in_specs=placed,
        out_specs=(P(("roll", "rep")), P(("roll", "rep")), P("roll")),
        check_vma=False,
    )
```

time: 341 us -> 397 us (1.16)
  waiting for transfers between devices: 155 us -> 243 us
  Pallas kernels: 0 us -> 58.8 us
  other arithmetic: 59.1 us -> 5.97 us
  starting transfers between devices: 52.4 us -> 0.16 us
  blocking collectives: 36.4 us -> 61.4 us
  local copies, waits for them, and re-layouts: 25.6 us -> 5.07 us
  between operations: 1.03 us -> 14.6 us
  matrix products: 10.6 us -> 3.42 us
    psum x0 -> x2, waiting for transfers between devices: none -> 172 us  [body(): demo_pot = SHIFT - jnp.log2(lax.psum(sums, 'roll') + FLOOR)]
    all_to_all x4 -> x0, waiting for transfers between devices: 155 us -> none  [the longest x1 136 us: body(): lax.all_to_all(outgoing.reshape(owners_n, capacity, block_len, features),...]
    all_gather x0 -> x2, waiting for transfers between devices: none -> 70.1 us  [the longest x1 70.1 us: body(): v = lax.all_gather(own_v, 'roll', tiled=True)]
    pallas_call x0 -> x4, Pallas kernels: none -> 58.8 us  [run_pass(): pl.pallas_call(functools.partial(pass_kernel, kind), out_shape=out, in_sp...]
    all_to_all x4 -> x0, starting transfers between devices: 52.4 us -> none  [the longest x1 36.5 us: body(): lax.all_to_all(column_lse.reshape(owners_n, capacity, block_len), 'roll',...]
    reduce_sum x10 -> x4, other arithmetic: 26.9 us -> 1.11 us  [the longest x1 0.66 us: listed(): total = jnp.sum(mine.astype(jnp.int32)).reshape(1)]
    all_gather x4, blocking collectives: 17.4 us -> 37 us  [the longest x1 23.7 us: body(): vnorm = lax.all_gather(norms(own_v, blk), 'roll', tiled=True)]
    psum x0 -> x2, blocking collectives: none -> 19.2 us  [body(): sums = lax.psum(sums, 'rep')]
  transfers between devices with their start and end apart: 4 -> 4, of which waited for: 4 -> 3; matrix products, arithmetic and copies ran while one was open for 5% -> 1% of each run, Pallas kernels for 0% -> 0%
where the time goes in v1:
time: 397 us; the launch traced here: 392 us
  waiting for transfers between devices  243 us (61%)
  blocking collectives  61.4 us (15%)
  Pallas kernels  58.8 us (15%)
  between operations  14.6 us (4%)
  other arithmetic  5.97 us (2%)
  local copies, waits for them, and re-layouts  5.07 us (1%)
    psum x2, waiting for transfers between devices, body(): demo_pot = SHIFT - jnp.log2(lax.psum(sums, 'roll') + FLOOR)  172 us
    all_gather x1, waiting for transfers between devices, body(): v = lax.all_gather(own_v, 'roll', tiled=True)  70.1 us
    pallas_call x4, Pallas kernels, run_pass(): pl.pallas_call(functools.partial(pass_kernel, kind), out_shape=out, in_sp...  58.8 us
    all_gather x1, blocking collectives, body(): vnorm = lax.all_gather(norms(own_v, blk), 'roll', tiled=True)  23.7 us
    psum x2, blocking collectives, body(): sums = lax.psum(sums, 'rep')  19.2 us
  transfers between devices with their start and end apart: 4, of which 3 were waited for; matrix products, arithmetic and copies ran while one was open for 1% of the time, Pallas kernels for 0%

profile of v1, /device:TPU:0, one launch (start us, length us, event | category | flops | bytes accessed | tf_op | source)
XLA Modules:
  0.0 392.0 jit_solution(3211119494691440315)
XLA Ops:
  7.3 1.5 copy-done
  8.8 2.3 multiply_reduce_fusion
  11.2 1.1 multiply_reduce_fusion.1
  12.4 0.6 dynamic-slice.2
  13.6 0.2 dynamic-update-slice
  13.9 5.2 %all-reduce.2 = s32[32]{0:T(128)S(1)} all-reduce(s32[32]{0:T(128)S(1)} %dynamic-update-slice), channel_id=1, replica_groups=mesh['roll'=16,'rep'=2] {'rep'}, use_global_device_ids=true, to_apply=%add.2 | all-reduce | flops 32 | bytes 256
  19.3 4.3 %all-gather = s32[2,16,8]{1,2,0:T(8,128)S(1)} all-gather(s32[1,16,8]{1,2,0:T(8,128)S(1)} %bitcast.17), channel_id=1, replica_groups=mesh['roll'=16,'rep'=2] {'rep'}, dimensions={0}, use_global_device_ids=true | all-gather | bytes 1536 | tf_op jit(solution)/shard_map/all_gather | solution.py:172
  23.8 0.2 select_reduce_fusion.2
  24.0 0.7 convert_reduce_fusion.1
  24.6 0.1 convert_reduce_fusion
  24.7 0.2 select_reduce_fusion
  24.9 0.6 pad.7.home_ref
  25.5 0.6 pad.8.target_ref
  26.1 4.6 %all_gather.25.unorm_ref = f32[32,128]{1,0:T(8,128)} all-gather(f32[16,128]{1,0:T(8,128)S(1)} %bitcast.16), channel_id=1, replica_groups=mesh['roll'=16,'rep'=2] {'rep'}, dimensions={0}, use_global_device_ids=true | all-gather | bytes 24576 | tf_op jit(solution)/shard_map/all_gather | solution.py:185
  30.7 23.7 %all_gather.26.vnorm_ref = f32[128,128]{1,0:T(8,128)} all-gather(f32[8,128]{1,0:T(8,128)S(1)} %bitcast.18), channel_id=1, replica_groups=mesh['roll'=16,'rep'=2] {'roll'}, dimensions={0}, use_global_device_ids=true | all-gather | bytes 69632 | tf_op jit(solution)/shard_map/all_gather | solution.py:183
  54.4 70.1 %all-gather.6.cloned.1.call-done.v_ref = bf16[16384,256]{1,0:T(8,128)(2,1)} async-done(((bf16[1024,256]{1,0:T(8,128)(2,1)}), bf16[16384,256]{1,0:T(8,128)(2,1)}) %all-gather.6.cloned.1.call-update) | async-done | bytes 8388624 | tf_op jit(solution)/shard_map/all_gather | solution.py:182
  124.4 0.6 broadcast_in_dim.44.pot_ref
  125.0 12.9 %pass_column.2 = f32[128,128]{1,0:T(8,128)} custom-call(s32[1]{0:T(128)} %bitcast.2.total_ref, s32[260]{0:T(512)} %pad.7.home_ref, s32[260]{0:T(512)} %pad.8.target_ref, bf16[4096,256]{1,0:T(8,128)(2,1)} %all-gather.4.cloned.1.call-done.u_ref, bf16[16384,256]{1,0:T(8,128)(2,1)} %all-gather.6.cloned.1.call-done.v_ref, f32[32,128]{1,0:T(8,128)} %all_gather.25.unorm_ref, ...), custom_call_target="tpu_custom_call" | custom-call | flops 1090519040 | bytes 10485760 | tf_op jit(solution)/shard_map/pass_column/pallas_call | solution.py:119
  138.0 85.8 %all-reduce.6.cloned.1.call-done = f32[128,128]{1,0:T(8,128)} async-done(((f32[128,128]{1,0:T(8,128)}), f32[128,128]{1,0:T(8,128)}) %all-reduce.6.cloned.1.call-update) | async-done | bytes 65552 | tf_op jit(solution)/shard_map/psum | solution.py:190
  223.9 1.5 multiply_subtract_fusion.1.pot_ref
  225.3 16.4 %pass_row.1 = f32[1,32,128]{2,1,0:T(8,128)} custom-call(s32[1]{0:T(128)} %bitcast.2.total_ref, s32[260]{0:T(512)} %pad.7.home_ref, s32[260]{0:T(512)} %pad.8.target_ref, bf16[4096,256]{1,0:T(8,128)(2,1)} %all-gather.4.cloned.1.call-done.u_ref, bf16[16384,256]{1,0:T(8,128)(2,1)} %all-gather.6.cloned.1.call-done.v_ref, f32[32,128]{1,0:T(8,128)} %all_gather.25.unorm_ref, ...), custom_call_target="tpu_custom_call" | custom-call | flops 1090519040 | bytes 10485760 | tf_op jit(solution)/shard_map/pass_row/pallas_call | solution.py:119
  241.7 9.5 %psum.29 = f32[1,32,128]{2,1,0:T(8,128)S(1)} all-reduce(f32[1,32,128]{2,1,0:T(8,128)} %pass_row.1), channel_id=1, replica_groups=mesh['roll'=16,'rep'=2] {'rep'}, use_global_device_ids=true, to_apply=%region_8.9 | all-reduce | flops 4096 | bytes 32768 | tf_op jit(solution)/shard_map/psum | solution.py:193
  251.2 0.6 subtract_bitcast_fusion.pot_ref
  251.9 12.9 %pass_column.3 = f32[128,128]{1,0:T(8,128)} custom-call(s32[1]{0:T(128)} %bitcast.2.total_ref, s32[260]{0:T(512)} %pad.7.home_ref, s32[260]{0:T(512)} %pad.8.target_ref, bf16[4096,256]{1,0:T(8,128)(2,1)} %all-gather.4.cloned.1.call-done.u_ref, bf16[16384,256]{1,0:T(8,128)(2,1)} %all-gather.6.cloned.1.call-done.v_ref, f32[32,128]{1,0:T(8,128)} %all_gather.25.unorm_ref, ...), custom_call_target="tpu_custom_call" | custom-call | flops 1090519040 | bytes 10485760 | tf_op jit(solution)/shard_map/pass_column/pallas_call | solution.py:119
  264.8 86.5 %all-reduce.8.cloned.1.call-done = f32[128,128]{1,0:T(8,128)} async-done(((f32[128,128]{1,0:T(8,128)}), f32[128,128]{1,0:T(8,128)}) %all-reduce.8.cloned.1.call-update) | async-done | bytes 65552 | tf_op jit(solution)/shard_map/psum | solution.py:190
  351.3 1.5 multiply_subtract_fusion.pot_ref
  352.8 16.7 %pass_final.1 = f32[2,32,128]{2,1,0:T(8,128)} custom-call(s32[1]{0:T(128)} %bitcast.2.total_ref, s32[260]{0:T(512)} %pad.7.home_ref, s32[260]{0:T(512)} %pad.8.target_ref, bf16[4096,256]{1,0:T(8,128)(2,1)} %all-gather.4.cloned.1.call-done.u_ref, bf16[16384,256]{1,0:T(8,128)(2,1)} %all-gather.6.cloned.1.call-done.v_ref, f32[32,128]{1,0:T(8,128)} %all_gather.25.unorm_ref, ...), custom_call_target="tpu_custom_call" | custom-call | flops 1090519040 | bytes 10485760 | tf_op jit(solution)/shard_map/pass_final/pallas_call | solution.py:119
  369.5 9.7 %psum.31 = f32[2,32,128]{2,1,0:T(8,128)S(1)} all-reduce(f32[2,32,128]{2,1,0:T(8,128)} %pass_final.1), channel_id=1, replica_groups=mesh['roll'=16,'rep'=2] {'rep'}, use_global_device_ids=true, to_apply=%region_10.11 | all-reduce | flops 8192 | bytes 65536 | tf_op jit(solution)/shard_map/psum | solution.py:193
  379.2 0.7 constant_dynamic-slice_fusion
  379.9 4.3 %all_gather.27 = f32[16,128]{1,0:T(8,128)S(1)} all-gather(f32[8,128]{1,0:T(8,128)S(1)} %constant_dynamic-slice_fusion), channel_id=1, replica_groups=mesh['roll'=16,'rep'=2] {'rep'}, dimensions={0}, use_global_device_ids=true | all-gather | bytes 12288 | tf_op jit(solution)/shard_map/all_gather | solution.py:198
  384.2 0.6 multiply_bitcast_fusion.1
  384.8 0.6 multiply_bitcast_fusion
  (29 shorter events, 0.6 us)
Async XLA Ops:
  7.2 1.6 copy-start
  7.2 5.2 %copy-start.6 = (u32[32]{0:T(128)S(1)}, u32[32]{0:T(128)}, u32[]{:S(2)}) copy-start(u32[32]{0:T(128)} %constant.106) | copy-start | bytes 388
  7.2 4.0 %copy-start.4 = (bf16[256,256]{1,0:T(8,128)(2,1)S(1)}, bf16[256,256]{1,0:T(8,128)(2,1)}, u32[]{:S(2)}) copy-start(bf16[256,256]{1,0:T(8,128)(2,1)} %param.8) | copy-start | bytes 393220
  7.2 4.0 %copy-start.3 = (bf16[2048,256]{1,0:T(8,128)(2,1)S(1)}, bf16[2048,256]{1,0:T(8,128)(2,1)}, u32[]{:S(2)}) copy-start(bf16[2048,256]{1,0:T(8,128)(2,1)} %param.7) | copy-start | bytes 3145732
  7.2 6.4 %copy-start.5 = (s32[16]{0:T(128)S(1)}, s32[16]{0:T(128)}, u32[]{:S(2)}) copy-start(s32[16]{0:T(128)} %param.11) | copy-start | bytes 196
  7.2 47.1 %all-gather.4.cloned.1.call-start = ((), (), s32[]{:S(2)}) async-start(), calls=%async_computation | async-start | bytes 3145728 | tf_op jit(solution)/shard_map/all_gather | solution.py:184
  11.1 8.2 %copy-start.1 = (s32[16,8]{0,1:T(8,128)S(1)}, s32[16,8]{0,1:T(8,128)}, u32[]{:S(2)}) copy-start(s32[16,8]{0,1:T(8,128)} %param.10) | copy-start | bytes 1540
  11.1 12.7 %copy-start.2 = (s32[256]{0:T(256)S(1)}, s32[256]{0:T(256)}, u32[]{:S(2)}) copy-start(s32[256]{0:T(256)} %param.9) | copy-start | bytes 3076
  11.1 113.3 %all-gather.6.cloned.1.call-start = ((), (), s32[]{:S(2)}) async-start(), calls=%async_computation.1 | async-start | bytes 8912896 | tf_op jit(solution)/shard_map/all_gather | solution.py:182
  12.3 211.5 %all-reduce.6.cloned.1.call-start = ((), (), s32[]{:S(2)}) async-start(), calls=%async_computation.2 | async-start | bytes 131072 | tf_op jit(solution)/shard_map/psum | solution.py:190
  138.0 213.3 %all-reduce.8.cloned.1.call-start = ((), (), s32[]{:S(2)}) async-start(), calls=%async_computation.3 | async-start | bytes 131072 | tf_op jit(solution)/shard_map/psum | solution.py:190
Sparse Core Ops, SparseCore 0:
  11.2 35.9 all-gather.3
  49.4 74.9 all-gather.5
  138.1 85.7 all-reduce.5
  264.9 86.3 all-reduce.7

commit v2 on v1

--- a/solution.py
+++ b/solution.py
@@ -16,6 +16,8 @@
 SHIFT = 50.0 * LOG2E
 FLOOR = math.exp(SLACK + 50.0)
 UNROLL = 4
+DIRECT = 16
+MESH = pl.DeviceIdType.MESH
 
 
 def pass_kernel(kind, total_ref, home_ref, target_ref, u_ref, v_ref, unorm_ref, vnorm_ref, pot_ref, *rest):
@@ -161,36 +163,266 @@
     return jnp.sum(wide * wide, axis=1).reshape(-1, blk)
 
 
+def greet(partners):
+    barrier = pltpu.get_barrier_semaphore()
+    for partner in partners:
+        pl.semaphore_signal(barrier, inc=1, device_id=partner, device_id_type=MESH)
+    pl.semaphore_wait(barrier, len(partners))
+
+
+def others(axis, size):
+    me = lax.axis_index(axis)
+    return [{axis: lax.rem(me + d, size)} for d in range(1, size)]
+
+
+def gather_kernel(n, reps, *refs):
+    own_v, own_vnorm, own_u, own_unorm, own_pairs = refs[:5]
+    v, vnorm, u, unorm, pairs = refs[5:10]
+    ring_send, ring_recv, side_send, side_recv, norm_send, norm_recv, rep_send, rep_recv, home = refs[10:]
+    me = lax.axis_index("roll")
+    part = lax.axis_index("rep")
+    chips = n // 2
+    hops = chips // 2
+    core = lax.rem(me, 2)
+    chip = me // 2
+    odd = lax.rem(chip, 2)
+    place = (1 - odd) * (chip // 2) + odd * (chips - 1 - chip // 2)
+
+    def at_place(p):
+        p = lax.rem(p + 2 * chips, chips)
+        high = p // hops
+        return ((1 - high) * (2 * p) + high * (2 * (chips - 1 - p) + 1)) * 2 + core
+
+    twin = {"roll": me + 1 - 2 * core}
+    ways = ({"roll": at_place(place + 1)}, {"roll": at_place(place - 1)})
+    rows = own_v.shape[0] // 2
+    greet(others("roll", n) + others("rep", reps))
+
+    waits = []
+    arrivals = []
+
+    def origin(way, s):
+        return at_place(place - s) if way == 0 else at_place(place + s)
+
+    def chunk(s, way, half):
+        piece = pl.ds(half * rows, rows)
+        if s == 0:
+            return own_v.at[piece], v.at[me, piece]
+        block = origin(way, s)
+        return v.at[block, piece], v.at[block, piece]
+
+    def send(s, way, half):
+        source, target = chunk(s, way, half)
+        copy = pltpu.make_async_remote_copy(
+            src_ref=source, dst_ref=target,
+            send_sem=ring_send.at[way, s, half], recv_sem=ring_recv.at[way, s, half],
+            device_id=ways[way], device_id_type=MESH,
+        )
+        copy.start()
+        return copy
+
+    def cross(s, way, half):
+        source, target = chunk(s, way, half)
+        copy = pltpu.make_async_remote_copy(
+            src_ref=source, dst_ref=target,
+            send_sem=side_send.at[way, s, half], recv_sem=side_recv.at[way, s, half],
+            device_id=twin, device_id_type=MESH,
+        )
+        copy.start()
+        waits.append(copy)
+
+    def travels(s, way, half):
+        return s < hops - 1 or (s == hops - 1 and half == way)
+
+    moving = {}
+    for half in range(2):
+        for way in range(2):
+            if travels(0, way, half):
+                moving[0, way, half] = send(0, way, half)
+    for source, targets, axis, which, sends, recvs in (
+        (own_pairs, pairs, "rep", 0, rep_send, rep_recv),
+        (own_unorm, unorm, "rep", 1, rep_send, rep_recv),
+        (own_u, u, "rep", 2, rep_send, rep_recv),
+        (own_vnorm, vnorm, "roll", 0, norm_send, norm_recv),
+    ):
+        index = part if axis == "rep" else me
+        for d, partner in enumerate(others(axis, reps if axis == "rep" else n)):
+            copy = pltpu.make_async_remote_copy(
+                src_ref=source, dst_ref=targets.at[index],
+                send_sem=sends.at[which, d], recv_sem=recvs.at[which, d],
+                device_id=partner, device_id_type=MESH,
+            )
+            copy.start()
+            waits.append(copy)
+    for half in range(2):
+        cross(0, 0, half)
+    stays = []
+    for k, (source, target) in enumerate(
+        ((own_v, v.at[me]), (own_vnorm, vnorm.at[me]), (own_u, u.at[part]), (own_unorm, unorm.at[part]), (own_pairs, pairs.at[part]))
+    ):
+        copy = pltpu.make_async_copy(source, target, home.at[k])
+        copy.start()
+        stays.append(copy)
+    for s in range(1, hops + 1):
+        for half in range(2):
+            for way in range(2):
+                if (s - 1, way, half) not in moving:
+                    continue
+                moving[s - 1, way, half].wait_recv()
+                if travels(s, way, half):
+                    moving[s, way, half] = send(s, way, half)
+                cross(s, way, half)
+    for copy in moving.values():
+        copy.wait_send()
+    for copy in stays:
+        copy.wait()
+    for copy in waits:
+        copy.wait()
+
+
+def gathered(n, reps, own_v, own_vnorm, own_u, own_unorm, own_pairs):
+    hops = n // 4
+    own = (own_v, own_vnorm, own_u, own_unorm, own_pairs)
+    counts = (n, n, reps, reps, reps)
+    anywhere = pl.BlockSpec(memory_space=pl.ANY)
+    dma = pltpu.SemaphoreType.DMA
+    return pl.pallas_call(
+        functools.partial(gather_kernel, n, reps),
+        out_shape=[jax.ShapeDtypeStruct((c,) + a.shape, a.dtype) for c, a in zip(counts, own)],
+        in_specs=[anywhere] * 5,
+        out_specs=[anywhere] * 5,
+        scratch_shapes=[
+            dma((2, hops, 2)), dma((2, hops, 2)),
+            dma((2, hops + 1, 2)), dma((2, hops + 1, 2)),
+            dma((1, n - 1)), dma((1, n - 1)),
+            dma((3, reps - 1)), dma((3, reps - 1)),
+            dma((5,)),
+        ],
+        compiler_params=pltpu.CompilerParams(collective_id=0, has_side_effects=True),
+        name="gather_codes",
+    )(*own)
+
+
+def column_kernel(n, sums, out, landed, full, first_send, first_recv, second_send, second_recv):
+    me = lax.axis_index("roll")
+    partners = others("roll", n)
+    greet(partners)
+    copies = []
+    for d, partner in enumerate(partners):
+        copy = pltpu.make_async_remote_copy(
+            src_ref=sums.at[partner["roll"]], dst_ref=landed.at[d],
+            send_sem=first_send.at[d], recv_sem=first_recv.at[d],
+            device_id=partner, device_id_type=MESH,
+        )
+        copy.start()
+        copies.append(copy)
+    total = sums[me]
+    for d, copy in enumerate(copies):
+        copy.wait_recv()
+        total = total + landed[d]
+    full[me] = SHIFT - jnp.log2(total + FLOOR)
+    seconds = []
+    for d, partner in enumerate(partners):
+        copy = pltpu.make_async_remote_copy(
+            src_ref=full.at[me], dst_ref=full.at[me],
+            send_sem=second_send.at[d], recv_sem=second_recv.at[d],
+            device_id=partner, device_id_type=MESH,
+        )
+        copy.start()
+        seconds.append(copy)
+    for copy in copies:
+        copy.wait_send()
+    for copy in seconds:
+        copy.wait()
+    out[...] = full[...]
+
+
+def column_potentials(n, sums, call):
+    if n > DIRECT:
+        return SHIFT - jnp.log2(lax.psum(sums, "roll") + FLOOR)
+    share, blk = sums.shape[0] // n, sums.shape[1]
+    sums = sums.reshape(n, share, blk)
+    dma = pltpu.SemaphoreType.DMA((n - 1,))
+    vmem = pl.BlockSpec(memory_space=pltpu.VMEM)
+    out = pl.pallas_call(
+        functools.partial(column_kernel, n),
+        out_shape=jax.ShapeDtypeStruct(sums.shape, sums.dtype),
+        in_specs=[vmem],
+        out_specs=vmem,
+        scratch_shapes=[
+            pltpu.VMEM((n - 1, share, blk), jnp.float32),
+            pltpu.VMEM((n, share, blk), jnp.float32),
+            dma, dma, dma, dma,
+        ],
+        compiler_params=pltpu.CompilerParams(collective_id=1 + call, has_side_effects=True),
+        name="column_exchange_%d" % call,
+    )(sums)
+    return out.reshape(n * share, blk)
+
+
+def row_kernel(reps, sums, out, landed, send_sem, recv_sem):
+    partners = others("rep", reps)
+    greet(partners)
+    copies = []
+    for d, partner in enumerate(partners):
+        copy = pltpu.make_async_remote_copy(
+            src_ref=sums, dst_ref=landed.at[d], send_sem=send_sem.at[d], recv_sem=recv_sem.at[d],
+            device_id=partner, device_id_type=MESH,
+        )
+        copy.start()
+        copies.append(copy)
+    total = sums[...]
+    for d, copy in enumerate(copies):
+        copy.wait_recv()
+        total = total + landed[d]
+    out[...] = total
+    for copy in copies:
+        copy.wait_send()
+
+
+def row_totals(reps, sums, call):
+    dma = pltpu.SemaphoreType.DMA((reps - 1,))
+    vmem = pl.BlockSpec(memory_space=pltpu.VMEM)
+    return pl.pallas_call(
+        functools.partial(row_kernel, reps),
+        out_shape=jax.ShapeDtypeStruct(sums.shape, sums.dtype),
+        in_specs=[vmem],
+        out_specs=vmem,
+        scratch_shapes=[pltpu.VMEM((reps - 1,) + sums.shape, jnp.float32), dma, dma],
+        compiler_params=pltpu.CompilerParams(collective_id=3 + call, has_side_effects=True),
+        name="row_exchange_%d" % call,
+    )(sums)
+
+
 def body(rollout, demo, projection, location, pair_block, pair_count):
-    own_blocks = pair_block.shape[0]
+    own_blocks, slots = pair_block.shape
     blk = rollout.shape[0] // own_blocks
     demo_count = demo.shape[0] // blk
+    n = lax.axis_size("roll")
     reps = lax.axis_size("rep")
     part = lax.axis_index("rep")
     share = demo_count // reps
-    lists = listed(
-        lax.all_gather(pair_block, "rep", tiled=True),
-        lax.all_gather(pair_count, "rep", tiled=True),
-        location,
-        demo_count,
-        share,
-        part,
-    )
     own_demo = lax.dynamic_slice_in_dim(demo, part * (share * blk), share * blk, 0)
     own_v = project(own_demo, projection)
     own_u = project(rollout, projection)
-    v = lax.all_gather(own_v, "roll", tiled=True)
-    vnorm = lax.all_gather(norms(own_v, blk), "roll", tiled=True)
-    u = lax.all_gather(own_u, "rep", tiled=True)
-    unorm = lax.all_gather(norms(own_u, blk), "rep", tiled=True)
+    own_pairs = jnp.concatenate([pair_block, pair_count[:, None]], axis=1)
+    own_pairs = jnp.pad(own_pairs, ((0, 0), (0, 128 - own_pairs.shape[1])))
+    own = (own_v, norms(own_v, blk), own_u, norms(own_u, blk), own_pairs)
+    if n <= DIRECT:
+        v, vnorm, u, unorm, pairs = gathered(n, reps, *own)
+    else:
+        v, vnorm = (lax.all_gather(a, "roll") for a in own[:2])
+        u, unorm, pairs = (lax.all_gather(a, "rep") for a in own[2:])
+    v, vnorm, u, unorm, pairs = (a.reshape(-1, a.shape[-1]) for a in (v, vnorm, u, unorm, pairs))
+    lists = listed(pairs[:, :slots], pairs[:, slots], location, demo_count, share, part)
 
     roll_pot = jnp.zeros_like(unorm)
     for iteration in range(2):
         sums = run_pass("column", lists, u, v, unorm, vnorm, roll_pot)
-        demo_pot = SHIFT - jnp.log2(lax.psum(sums, "roll") + FLOOR)
+        demo_pot = column_potentials(n, sums, iteration)
         kind = "final" if iteration == 1 else "row"
         sums = run_pass(kind, lists, u, v, unorm, vnorm, demo_pot)
-        sums = lax.psum(sums, "rep")
+        sums = row_totals(reps, sums, iteration)
         heights = sums[0] + FLOOR
         roll_pot = SHIFT - jnp.log2(heights)
     reward = -(sums[1] + UNMATCHED * FLOOR) / heights

time: 397 us -> 182 us (0.46); the launches traced: 392 us -> 182 us
  waiting for transfers between devices: 243 us -> 0 us
  Pallas kernels: 58.8 us -> 162 us
  blocking collectives: 61.4 us -> 4.33 us
  between operations: 14.6 us -> 0.74 us
    psum x2 -> x0, waiting for transfers between devices: 172 us -> none  [body(): demo_pot = SHIFT - jnp.log2(lax.psum(sums, 'roll') + FLOOR)]
    pallas_call x0 -> x5, Pallas kernels: none -> 102 us  [the longest x1 56.5 us: gathered(): pl.pallas_call(functools.partial(gather_kernel, n, reps), out_shape=[jax....]
    all_gather x2 -> x0, waiting for transfers between devices: 70.1 us -> none  [the longest x1 70.1 us: body(): v = lax.all_gather(own_v, 'roll', tiled=True)]
    all_gather x3 -> x0, blocking collectives: 32.6 us -> none  [the longest x1 23.7 us: body(): vnorm = lax.all_gather(norms(own_v, blk), 'roll', tiled=True)]
    psum x2 -> x0, blocking collectives: 19.2 us -> none  [body(): sums = lax.psum(sums, 'rep')]
    unnamed x1 -> x0, blocking collectives: 5.19 us -> none
  transfers between devices with their start and end apart: 4 -> 0, of which waited for: 3 -> 0; matrix products, arithmetic and copies ran while one was open for 1% -> 0% of each run, Pallas kernels for 0% -> 0%
where the time goes in v2:
time: 182 us
  Pallas kernels  162 us (89%)
  matrix products  5.75 us (3%)
  local copies, waits for them, and re-layouts  5.03 us (3%)
  other arithmetic  4.55 us (2%)
  blocking collectives  4.33 us (2%)
    pallas_call x4, Pallas kernels, run_pass(): pl.pallas_call(functools.partial(pass_kernel, kind), out_shape=out, in_sp...  59.9 us
    pallas_call x1, Pallas kernels, gathered(): pl.pallas_call(functools.partial(gather_kernel, n, reps), out_shape=[jax....  56.5 us
    pallas_call x2, Pallas kernels, column_potentials(): pl.pallas_call(functools.partial(column_kernel, n), out_shape=jax.ShapeDt...  34.9 us
    pallas_call x2, Pallas kernels, row_totals(): pl.pallas_call(functools.partial(row_kernel, reps), out_shape=jax.ShapeDt...  10.4 us
    dot_general x2, matrix products, project(): jnp.dot(frames, projection, preferred_element_type=jnp.float32)  5.75 us
    all_gather x1, blocking collectives, body(): lax.all_gather(lax.dynamic_slice_in_dim(demo_pot, mine, share, 0), 'rep',...  4.33 us

profile of v2, /device:TPU:0, one launch (start us, length us, event | category | flops | bytes accessed | tf_op | source)
XLA Modules:
  0.0 182.0 jit_solution(5622822196334766393)
XLA Ops:
  0.7 2.8 %multiply_reduce_fusion.1 = (f32[1024]{0:T(1024)}, bf16[1024,256]{1,0:T(8,128)(2,1)}) fusion(bf16[256,256]{1,0:T(8,128)(2,1)} %param.8, bf16[2048,256]{1,0:T(8,128)(2,1)} %param.7, s32[]{:T(128)S(6)} %select_n.87), kind=kOutput, calls=%fused_computation.3 | convolution fusion | flops 135265280 | bytes 1183748 | tf_op jit(solution)/shard_map/dot_general | solution.py:158
  3.5 2.9 %multiply_reduce_fusion = (f32[2048]{0:T(1024)}, bf16[2048,256]{1,0:T(8,128)(2,1)}) fusion(bf16[2048,256]{1,0:T(8,128)(2,1)S(1)} %copy-done, bf16[256,256]{1,0:T(8,128)(2,1)} %param.8), kind=kOutput, calls=%fused_computation.1 | convolution fusion | flops 270530560 | bytes 2236416 | tf_op jit(solution)/shard_map/dot_general | solution.py:158
  6.4 0.1 copy.24
  6.5 0.1 copy.25
  6.6 0.1 pad_add_fusion
  6.7 0.6 pad.11.refs_4_
  7.3 56.5 %gather_codes.1 = (bf16[16,1024,256]{2,1,0:T(8,128)(2,1)}, f32[16,8,128]{2,1,0:T(8,128)}, bf16[2,2048,256]{2,1,0:T(8,128)(2,1)}, f32[2,16,128]{2,1,0:T(8,128)}, s32[2,16,128]{2,1,0:T(8,128)}) custom-call(bf16[1024,256]{1,0:T(8,128)(2,1)} %get-tuple-element.23.refs_0_, f32[8,128]{1,0:T(8,128)} %bitcast.49, bf16[2048,256]{1,0:T(8,128)(2,1)} %get-tuple-element.25.refs_2_, ...), custom_call_target="tpu_custom_call" | custom-call | tf_op jit(solution)/shard_map/gather_codes/pallas_call | solution.py:289
  63.8 0.9 slice_reduce_fusion
  64.7 0.1 iota_compare_fusion.3
  64.8 0.1 lt.68
  64.9 0.8 eq.48
  65.7 0.2 select_reduce_fusion.2
  65.9 0.7 convert_reduce_fusion.1
  66.6 0.1 convert_reduce_fusion
  66.7 0.2 select_reduce_fusion
  66.9 0.6 pad.12.home_ref
  67.4 0.6 pad.13.target_ref
  68.0 0.6 broadcast_in_dim.47.pot_ref
  68.6 13.2 %pass_column.2 = f32[128,128]{1,0:T(8,128)} custom-call(s32[1]{0:T(128)} %bitcast.4.total_ref, s32[260]{0:T(512)} %pad.12.home_ref, s32[260]{0:T(512)} %pad.13.target_ref, bf16[4096,256]{1,0:T(8,128)(2,1)} %bitcast.29, bf16[16384,256]{1,0:T(8,128)(2,1)} %bitcast.25, f32[32,128]{1,0:T(8,128)} %bitcast.39, f32[128,128]{1,0:T(8,128)} %bitcast.33, ...), custom_call_target="tpu_custom_call" | custom-call | flops 1090519040 | bytes 10485760 | tf_op jit(solution)/shard_map/pass_column/pallas_call | solution.py:121
  81.8 15.1 %column_exchange_0.1 = f32[16,8,128]{2,1,0:T(8,128)} custom-call(f32[16,8,128]{2,1,0:T(8,128)} %bitcast.43), custom_call_target="tpu_custom_call" | custom-call | tf_op jit(solution)/shard_map/column_exchange_0/pallas_call | solution.py:347
  96.9 16.6 %pass_row.1.sums = f32[1,32,128]{2,1,0:T(8,128)} custom-call(s32[1]{0:T(128)} %bitcast.4.total_ref, s32[260]{0:T(512)} %pad.12.home_ref, s32[260]{0:T(512)} %pad.13.target_ref, bf16[4096,256]{1,0:T(8,128)(2,1)} %bitcast.30, bf16[16384,256]{1,0:T(8,128)(2,1)} %bitcast.26, f32[32,128]{1,0:T(8,128)} %bitcast.40, f32[128,128]{1,0:T(8,128)} %bitcast.34, ...), custom_call_target="tpu_custom_call" | custom-call | flops 1090519040 | bytes 10485760 | tf_op jit(solution)/shard_map/pass_row/pallas_call | solution.py:121
  113.5 5.1 %row_exchange_0.1 = f32[1,32,128]{2,1,0:T(8,128)} custom-call(f32[1,32,128]{2,1,0:T(8,128)} %pass_row.1.sums), custom_call_target="tpu_custom_call" | custom-call | tf_op jit(solution)/shard_map/row_exchange_0/pallas_call | solution.py:386
  118.6 1.3 subtract_bitcast_fusion.pot_ref
  119.9 13.1 %pass_column.3 = f32[128,128]{1,0:T(8,128)} custom-call(s32[1]{0:T(128)} %bitcast.4.total_ref, s32[260]{0:T(512)} %pad.12.home_ref, s32[260]{0:T(512)} %pad.13.target_ref, bf16[4096,256]{1,0:T(8,128)(2,1)} %bitcast.31, bf16[16384,256]{1,0:T(8,128)(2,1)} %bitcast.27, f32[32,128]{1,0:T(8,128)} %bitcast.41, f32[128,128]{1,0:T(8,128)} %bitcast.35, ...), custom_call_target="tpu_custom_call" | custom-call | flops 1090519040 | bytes 10485760 | tf_op jit(solution)/shard_map/pass_column/pallas_call | solution.py:121
  133.1 19.8 %column_exchange_1.1 = f32[16,8,128]{2,1,0:T(8,128)} custom-call(f32[16,8,128]{2,1,0:T(8,128)} %bitcast.45), custom_call_target="tpu_custom_call" | custom-call | tf_op jit(solution)/shard_map/column_exchange_1/pallas_call | solution.py:347
  152.9 16.9 %pass_final.1.sums = f32[2,32,128]{2,1,0:T(8,128)} custom-call(s32[1]{0:T(128)} %bitcast.4.total_ref, s32[260]{0:T(512)} %pad.12.home_ref, s32[260]{0:T(512)} %pad.13.target_ref, bf16[4096,256]{1,0:T(8,128)(2,1)} %bitcast.32, bf16[16384,256]{1,0:T(8,128)(2,1)} %bitcast.28, f32[32,128]{1,0:T(8,128)} %bitcast.42, f32[128,128]{1,0:T(8,128)} %bitcast.36, ...), custom_call_target="tpu_custom_call" | custom-call | flops 1090519040 | bytes 10485760 | tf_op jit(solution)/shard_map/pass_final/pallas_call | solution.py:121
  169.8 5.3 %row_exchange_1.1 = f32[2,32,128]{2,1,0:T(8,128)} custom-call(f32[2,32,128]{2,1,0:T(8,128)} %pass_final.1.sums), custom_call_target="tpu_custom_call" | custom-call | tf_op jit(solution)/shard_map/row_exchange_1/pallas_call | solution.py:386
  175.1 0.7 slice_add_fusion
  175.8 0.6 multiply_bitcast_fusion
  176.4 0.7 constant_dynamic-slice_fusion
  177.1 4.3 %all_gather.3 = f32[16,128]{1,0:T(8,128)S(1)} all-gather(f32[8,128]{1,0:T(8,128)S(1)} %constant_dynamic-slice_fusion), channel_id=1, replica_groups=mesh['roll'=16,'rep'=2] {'rep'}, dimensions={0}, use_global_device_ids=true | all-gather | bytes 12288 | tf_op jit(solution)/shard_map/all_gather | solution.py:430
  181.4 0.6 multiply_bitcast_fusion.1
  (9 shorter events, 0.0 us)
Async XLA Ops:
  0.6 2.9 %copy-start = (bf16[2048,256]{1,0:T(8,128)(2,1)S(1)}, bf16[2048,256]{1,0:T(8,128)(2,1)}, u32[]{:S(2)}) copy-start(bf16[2048,256]{1,0:T(8,128)(2,1)} %param.6) | copy-start | bytes 3145732
  0.6 5.8 %copy-start.1 = (s32[16,8]{0,1:T(8,128)S(1)}, s32[16,8]{0,1:T(8,128)}, u32[]{:S(2)}) copy-start(s32[16,8]{0,1:T(8,128)} %param.10) | copy-start | bytes 1540
  0.7 5.8 %copy-start.3 = (s32[16]{0:T(128)S(1)}, s32[16]{0:T(128)}, u32[]{:S(2)}) copy-start(s32[16]{0:T(128)} %param.11) | copy-start | bytes 196
  3.5 62.2 %copy-start.2 = (s32[256]{0:T(256)S(1)}, s32[256]{0:T(256)}, u32[]{:S(2)}) copy-start(s32[256]{0:T(256)} %param.9) | copy-start | bytes 3076

commit v3 on v2

--- a/solution.py
+++ b/solution.py
@@ -8,6 +8,7 @@
 from jax.experimental.pallas import tpu as pltpu
 from jax.sharding import PartitionSpec as P
 
+ITERS = 2
 EPSILON = 0.02
 UNMATCHED = 2.0
 SLACK = -100.0
@@ -17,10 +18,11 @@
 FLOOR = math.exp(SLACK + 50.0)
 UNROLL = 4
 DIRECT = 16
+MIB = 1024 * 1024
 MESH = pl.DeviceIdType.MESH
 
 
-def pass_kernel(kind, total_ref, home_ref, target_ref, u_ref, v_ref, unorm_ref, vnorm_ref, pot_ref, *rest):
+def pass_kernel(kind, first, lists_ref, u_ref, v_ref, unorm_ref, vnorm_ref, pot_ref, *rest):
     roll_blocks, blk = unorm_ref.shape
     feats = u_ref.shape[1]
     unit = SCALE / feats
@@ -38,22 +40,22 @@
     def prepare(b, carry):
         line = unorm_ref[pl.ds(b, 1), :] * (-unit)
         if kind == "column":
-            line = line + (pot_ref[pl.ds(b, 1), :] + SHIFT)
+            line = line + (SHIFT if first else pot_ref[pl.ds(b, 1), :] + SHIFT)
         row_term[pl.ds(b * blk, blk), :] = jnp.transpose(jnp.broadcast_to(line, (blk, blk)))
         return carry
 
-    lax.fori_loop(0, roll_blocks, prepare, 0)
+    lax.fori_loop(0, roll_blocks, prepare, 0, unroll=8)
     if kind != "column":
         col_term[...] = pot_ref[...] + SHIFT
 
-    total = total_ref[0]
+    total = lists_ref[2, 0]
 
     def step(k, carry):
         parts = []
         for p in range(UNROLL):
             at = k * UNROLL + p
-            b = home_ref[at]
-            t = target_ref[at]
+            b = lists_ref[0, at]
+            t = lists_ref[1, at]
             live = jnp.where(at < total, 0.0, -1e30)
             rows = pl.ds(pl.multiple_of(b * blk, blk), blk)
             crossed = lax.dot_general(
@@ -100,10 +102,10 @@
                 ) * (-1.0 / SCALE)
             return carry
 
-        lax.fori_loop(0, roll_blocks, finish, 0)
-
-
-def run_pass(kind, lists, u, v, unorm, vnorm, pot):
+        lax.fori_loop(0, roll_blocks, finish, 0, unroll=8)
+
+
+def run_pass(kind, first, lists, u, v, unorm, vnorm, pot):
     roll_blocks, blk = unorm.shape
     targets = vnorm.shape[0]
     smem = pl.BlockSpec(memory_space=pltpu.SMEM)
@@ -117,21 +119,22 @@
         scratch = [frames, pltpu.VMEM((targets, blk), jnp.float32), frames]
         if kind == "final":
             scratch.append(frames)
-    pairs = lists[1].shape[0] // 2
+    pairs = lists.shape[1] // 3
+    held = sum(math.prod(a.shape) * a.dtype.itemsize for a in [u, v, out] + scratch)
     return pl.pallas_call(
-        functools.partial(pass_kernel, kind),
+        functools.partial(pass_kernel, kind, first),
         out_shape=out,
-        in_specs=[smem] * 3 + [vmem] * 5,
+        in_specs=[smem] + [vmem] * 5,
         out_specs=vmem,
         scratch_shapes=scratch,
-        compiler_params=pltpu.CompilerParams(vmem_limit_bytes=56 * 1024 * 1024),
+        compiler_params=pltpu.CompilerParams(vmem_limit_bytes=held + 3 * MIB),
         cost_estimate=pl.CostEstimate(
             flops=2 * pairs * blk * blk * u.shape[1],
             bytes_accessed=2 * (u.size + v.size),
             transcendentals=pairs * blk * blk,
         ),
         name="pass_" + kind,
-    )(*lists, u, v, unorm, vnorm, pot)
+    )(lists, u, v, unorm, vnorm, pot)
 
 
 def listed(pair_block, pair_count, location, demo_count, share, part):
@@ -151,7 +154,8 @@
     home = jnp.sum(jnp.where(hit, (ids // slots)[None, :], 0), axis=1)
     target = jnp.sum(jnp.where(hit, target[None, :], 0), axis=1)
     total = jnp.sum(mine.astype(jnp.int32)).reshape(1)
-    return total, jnp.pad(home, (0, UNROLL)), jnp.pad(target, (0, UNROLL))
+    lists = jnp.stack([home, target, jnp.broadcast_to(total, (n,))])
+    return jnp.pad(lists, ((0, 0), (0, 128)))
 
 
 def project(frames, projection):
@@ -175,10 +179,56 @@
     return [{axis: lax.rem(me + d, size)} for d in range(1, size)]
 
 
-def gather_kernel(n, reps, *refs):
-    own_v, own_vnorm, own_u, own_unorm, own_pairs = refs[:5]
-    v, vnorm, u, unorm, pairs = refs[5:10]
-    ring_send, ring_recv, side_send, side_recv, norm_send, norm_recv, rep_send, rep_recv, home = refs[10:]
+def block_norms(codes):
+    wide = codes.astype(jnp.float32)
+    square = wide * wide
+    high = square.astype(jnp.bfloat16)
+    low = (square - high.astype(jnp.float32)).astype(jnp.bfloat16)
+    ones = jnp.ones((8, codes.shape[1]), jnp.bfloat16)
+    dims = (((1,), (1,)), ((), ()))
+    total = lax.dot_general(ones, high, dims, preferred_element_type=jnp.float32)
+    total = total + lax.dot_general(ones, low, dims, preferred_element_type=jnp.float32)
+    return total[0:1, :]
+
+
+def packed_pairs(pairs, location, slots, demo_count, share, part, width):
+    blocks = pairs.shape[0]
+    names = lax.broadcasted_iota(jnp.int32, (blocks, location.shape[1]), 1)
+    places = lax.broadcasted_iota(jnp.int32, (blocks, width), 1).astype(jnp.float32)
+    number = lax.broadcasted_iota(jnp.int32, (blocks, width), 0).astype(jnp.float32)
+    count = pairs[:, slots : slots + 1]
+    where_held = location.astype(jnp.float32)
+    mine, target = [], []
+    for s in range(slots):
+        hit = pairs[:, s : s + 1] == names
+        stored = jnp.sum(jnp.where(hit, where_held, 0.0), axis=1, keepdims=True)
+        owner = jnp.floor((stored + 0.5) * (1.0 / demo_count))
+        local = stored - owner * demo_count
+        side = jnp.floor((local + 0.5) * (1.0 / share))
+        mine.append(jnp.where((count > s) & (side == part.astype(jnp.float32)), 1.0, 0.0))
+        target.append(owner * share + local - side * share)
+    in_row = sum(mine)
+    below = lax.broadcasted_iota(jnp.int32, (blocks, blocks), 1) < lax.broadcasted_iota(jnp.int32, (blocks, blocks), 0)
+    spread = jnp.broadcast_to(in_row, (blocks, 128)).astype(jnp.bfloat16)
+    before = jnp.dot(below.astype(jnp.float32).astype(jnp.bfloat16), spread, preferred_element_type=jnp.float32)
+    rank = before[:, 0:1]
+    homes = jnp.zeros((blocks, width), jnp.float32)
+    targets = jnp.zeros((blocks, width), jnp.float32)
+    for s in range(slots):
+        hit = (rank == places) & (mine[s] > 0.5)
+        homes = homes + jnp.where(hit, number, 0.0)
+        targets = targets + jnp.where(hit, target[s], 0.0)
+        rank = rank + mine[s]
+    total = jnp.sum(jnp.broadcast_to(in_row, (blocks, width)), axis=0, keepdims=True)
+    rows = [jnp.sum(homes, axis=0, keepdims=True), jnp.sum(targets, axis=0, keepdims=True), total]
+    return [row.astype(jnp.int32) for row in rows]
+
+
+def gather_kernel(n, reps, slots, *refs):
+    demo, rollout, projection, own_pairs, location = refs[:5]
+    v, vnorm, u, unorm, lists = refs[5:10]
+    (demo_in, rollout_in, own_v, own_vnorm, own_u, own_unorm, pairs,
+     ring_send, ring_recv, side_send, side_recv, norm_send, norm_recv, rep_send, rep_recv, home) = refs[10:]
     me = lax.axis_index("roll")
     part = lax.axis_index("rep")
     chips = n // 2
@@ -196,10 +246,25 @@
     twin = {"roll": me + 1 - 2 * core}
     ways = ({"roll": at_place(place + 1)}, {"roll": at_place(place - 1)})
     rows = own_v.shape[0] // 2
-    greet(others("roll", n) + others("rep", reps))
+    share, blk = own_vnorm.shape
+    own_blocks = own_unorm.shape[0]
+    near = others("roll", n) + others("rep", reps)
+    fetch_demo = pltpu.make_async_copy(demo.at[pl.ds(part * (share * blk), share * blk)], demo_in, home.at[4])
+    fetch_demo.start()
+    fetch_rollout = pltpu.make_async_copy(rollout, rollout_in, home.at[5])
+    fetch_rollout.start()
+    barrier = pltpu.get_barrier_semaphore()
+    for partner in near:
+        pl.semaphore_signal(barrier, inc=1, device_id=partner, device_id_type=MESH)
+    fetch_demo.wait()
+    for half in range(2):
+        piece = pl.ds(half * rows, rows)
+        own_v[piece, :] = jnp.dot(
+            demo_in[piece, :], projection[...], preferred_element_type=jnp.float32
+        ).astype(jnp.bfloat16)
+    pl.semaphore_wait(barrier, len(near))
 
     waits = []
-    arrivals = []
 
     def origin(way, s):
         return at_place(place - s) if way == 0 else at_place(place + s)
@@ -239,30 +304,58 @@
         for way in range(2):
             if travels(0, way, half):
                 moving[0, way, half] = send(0, way, half)
-    for source, targets, axis, which, sends, recvs in (
-        (own_pairs, pairs, "rep", 0, rep_send, rep_recv),
-        (own_unorm, unorm, "rep", 1, rep_send, rep_recv),
-        (own_u, u, "rep", 2, rep_send, rep_recv),
-        (own_vnorm, vnorm, "roll", 0, norm_send, norm_recv),
-    ):
-        index = part if axis == "rep" else me
+
+    def spread(source, target, axis, which, sends, recvs):
+        started = []
         for d, partner in enumerate(others(axis, reps if axis == "rep" else n)):
             copy = pltpu.make_async_remote_copy(
-                src_ref=source, dst_ref=targets.at[index],
+                src_ref=source, dst_ref=target,
                 send_sem=sends.at[which, d], recv_sem=recvs.at[which, d],
                 device_id=partner, device_id_type=MESH,
             )
             copy.start()
-            waits.append(copy)
+            started.append(copy)
+        return started
+
+    pair_copies = spread(own_pairs, pairs.at[part], "rep", 0, rep_send, rep_recv)
+    pairs[part] = own_pairs[...]
     for half in range(2):
         cross(0, 0, half)
+    fetch_rollout.wait()
+
+    def do_rollout(b, carry):
+        rows_b = pl.ds(pl.multiple_of(b * blk, blk), blk)
+        codes = jnp.dot(
+            rollout_in[rows_b, :], projection[...], preferred_element_type=jnp.float32
+        ).astype(jnp.bfloat16)
+        own_u[rows_b, :] = codes
+        own_unorm[pl.ds(b, 1), :] = block_norms(codes)
+        return carry
+
+    lax.fori_loop(0, own_blocks, do_rollout, 0)
+    waits += spread(own_u, u.at[part], "rep", 1, rep_send, rep_recv)
+    waits += spread(own_unorm, unorm.at[part], "rep", 2, rep_send, rep_recv)
+
+    def do_demo(b, carry):
+        own_vnorm[pl.ds(b, 1), :] = block_norms(own_v[pl.ds(pl.multiple_of(b * blk, blk), blk), :])
+        return carry
+
+    lax.fori_loop(0, share, do_demo, 0)
+    waits += spread(own_vnorm, vnorm.at[me], "roll", 0, norm_send, norm_recv)
     stays = []
     for k, (source, target) in enumerate(
-        ((own_v, v.at[me]), (own_vnorm, vnorm.at[me]), (own_u, u.at[part]), (own_unorm, unorm.at[part]), (own_pairs, pairs.at[part]))
+        ((own_v, v.at[me]), (own_vnorm, vnorm.at[me]), (own_u, u.at[part]), (own_unorm, unorm.at[part]))
     ):
         copy = pltpu.make_async_copy(source, target, home.at[k])
         copy.start()
         stays.append(copy)
+    for copy in pair_copies:
+        copy.wait()
+    everyone = pairs[...].reshape(reps * own_blocks, pairs.shape[2])
+    found = packed_pairs(everyone, location[...], slots, share * reps, share, part, lists.shape[1])
+    lists[...] = jnp.zeros_like(lists)
+    for k, row in enumerate(found):
+        lists[k : k + 1, :] = row
     for s in range(1, hops + 1):
         for half in range(2):
             for way in range(2):
@@ -280,33 +373,59 @@
         copy.wait()
 
 
-def gathered(n, reps, own_v, own_vnorm, own_u, own_unorm, own_pairs):
+def gathered(n, reps, demo, rollout, projection, pair_block, pair_count, location):
     hops = n // 4
-    own = (own_v, own_vnorm, own_u, own_unorm, own_pairs)
-    counts = (n, n, reps, reps, reps)
+    own_blocks, slots = pair_block.shape
+    blk = rollout.shape[0] // own_blocks
+    feats = projection.shape[1]
+    share = demo.shape[0] // blk // reps
+    own_pairs = jnp.concatenate([pair_block, pair_count[:, None]], axis=1)
+    own_pairs = jnp.pad(own_pairs, ((0, 0), (0, 128 - own_pairs.shape[1])))
     anywhere = pl.BlockSpec(memory_space=pl.ANY)
+    vmem = pl.BlockSpec(memory_space=pltpu.VMEM)
     dma = pltpu.SemaphoreType.DMA
+    wide, code = jnp.float32, jnp.bfloat16
     return pl.pallas_call(
-        functools.partial(gather_kernel, n, reps),
-        out_shape=[jax.ShapeDtypeStruct((c,) + a.shape, a.dtype) for c, a in zip(counts, own)],
-        in_specs=[anywhere] * 5,
-        out_specs=[anywhere] * 5,
+        functools.partial(gather_kernel, n, reps, slots),
+        out_shape=[
+            jax.ShapeDtypeStruct((n, share * blk, feats), code),
+            jax.ShapeDtypeStruct((n, share, blk), wide),
+            jax.ShapeDtypeStruct((reps, own_blocks * blk, feats), code),
+            jax.ShapeDtypeStruct((reps, own_blocks, blk), wide),
+            jax.ShapeDtypeStruct((8, reps * own_blocks * slots + 128), jnp.int32),
+        ],
+        in_specs=[anywhere, anywhere, vmem, vmem, vmem],
+        out_specs=[anywhere] * 4 + [vmem],
         scratch_shapes=[
+            pltpu.VMEM((share * blk, feats), code),
+            pltpu.VMEM(rollout.shape, code),
+            pltpu.VMEM((share * blk, feats), code),
+            pltpu.VMEM((share, blk), wide),
+            pltpu.VMEM((own_blocks * blk, feats), code),
+            pltpu.VMEM((own_blocks, blk), wide),
+            pltpu.VMEM((reps,) + own_pairs.shape, jnp.int32),
             dma((2, hops, 2)), dma((2, hops, 2)),
             dma((2, hops + 1, 2)), dma((2, hops + 1, 2)),
             dma((1, n - 1)), dma((1, n - 1)),
             dma((3, reps - 1)), dma((3, reps - 1)),
-            dma((5,)),
+            dma((6,)),
         ],
-        compiler_params=pltpu.CompilerParams(collective_id=0, has_side_effects=True),
+        compiler_params=pltpu.CompilerParams(
+            collective_id=0, has_side_effects=True, vmem_limit_bytes=8 * MIB
+        ),
         name="gather_codes",
-    )(*own)
-
-
-def column_kernel(n, sums, out, landed, full, first_send, first_recv, second_send, second_recv):
+    )(demo, rollout, projection, own_pairs, location[None, :])
+
+
+def column_kernel(n, reps, sums, *refs):
+    if reps:
+        out, both, landed, full, held, first_send, first_recv, second_send, second_recv, rep_send, rep_recv = refs
+    else:
+        out, landed, full, first_send, first_recv, second_send, second_recv = refs
     me = lax.axis_index("roll")
     partners = others("roll", n)
-    greet(partners)
+    twins = others("rep", reps) if reps else []
+    greet(partners + twins)
     copies = []
     for d, partner in enumerate(partners):
         copy = pltpu.make_async_remote_copy(
@@ -320,7 +439,8 @@
     for d, copy in enumerate(copies):
         copy.wait_recv()
         total = total + landed[d]
-    full[me] = SHIFT - jnp.log2(total + FLOOR)
+    pot = SHIFT - jnp.log2(total + FLOOR)
+    full[me] = pot
     seconds = []
     for d, partner in enumerate(partners):
         copy = pltpu.make_async_remote_copy(
@@ -330,37 +450,64 @@
         )
         copy.start()
         seconds.append(copy)
+    if reps:
+        part = lax.axis_index("rep")
+        held[part] = pot * (1.0 / SCALE)
+        for d, partner in enumerate(twins):
+            copy = pltpu.make_async_remote_copy(
+                src_ref=held.at[part], dst_ref=held.at[part],
+                send_sem=rep_send.at[d], recv_sem=rep_recv.at[d],
+                device_id=partner, device_id_type=MESH,
+            )
+            copy.start()
+            seconds.append(copy)
     for copy in copies:
         copy.wait_send()
     for copy in seconds:
         copy.wait()
     out[...] = full[...]
-
-
-def column_potentials(n, sums, call):
+    if reps:
+        both[...] = held[...]
+
+
+def column_potentials(n, reps, sums, call):
+    last = call == ITERS - 1
+    share, blk = sums.shape[0] // n, sums.shape[1]
     if n > DIRECT:
-        return SHIFT - jnp.log2(lax.psum(sums, "roll") + FLOOR)
-    share, blk = sums.shape[0] // n, sums.shape[1]
+        pot = SHIFT - jnp.log2(lax.psum(sums, "roll") + FLOOR)
+        if not last:
+            return pot, None
+        mine = lax.dynamic_slice_in_dim(pot, lax.axis_index("roll") * share, share, 0)
+        return pot, lax.all_gather(mine, "rep") / SCALE
     sums = sums.reshape(n, share, blk)
-    dma = pltpu.SemaphoreType.DMA((n - 1,))
+    dma = pltpu.SemaphoreType.DMA
     vmem = pl.BlockSpec(memory_space=pltpu.VMEM)
+    both = (reps, share, blk)
+    outs = [jax.ShapeDtypeStruct(sums.shape, sums.dtype)]
+    scratch = [pltpu.VMEM((n - 1, share, blk), jnp.float32), pltpu.VMEM((n, share, blk), jnp.float32)]
+    if last:
+        outs.append(jax.ShapeDtypeStruct(both, sums.dtype))
+        scratch.append(pltpu.VMEM(both, jnp.float32))
+    scratch += [dma((n - 1,))] * 4
+    if last:
+        scratch += [dma((reps - 1,))] * 2
     out = pl.pallas_call(
-        functools.partial(column_kernel, n),
-        out_shape=jax.ShapeDtypeStruct(sums.shape, sums.dtype),
+        functools.partial(column_kernel, n, reps if last else 0),
+        out_shape=outs,
         in_specs=[vmem],
-        out_specs=vmem,
-        scratch_shapes=[
-            pltpu.VMEM((n - 1, share, blk), jnp.float32),
-            pltpu.VMEM((n, share, blk), jnp.float32),
-            dma, dma, dma, dma,
-        ],
-        compiler_params=pltpu.CompilerParams(collective_id=1 + call, has_side_effects=True),
+        out_specs=[vmem] * len(outs),
+        scratch_shapes=scratch,
+        compiler_params=pltpu.CompilerParams(
+            collective_id=1 + call, has_side_effects=True, vmem_limit_bytes=MIB
+        ),
         name="column_exchange_%d" % call,
     )(sums)
-    return out.reshape(n * share, blk)
-
-
-def row_kernel(reps, sums, out, landed, send_sem, recv_sem):
+    return out[0].reshape(n * share, blk), out[1] if last else None
+
+
+def row_kernel(reps, last, sums, *refs):
+    outs, (landed, send_sem, recv_sem) = refs[:-3], refs[-3:]
+    part = lax.axis_index("rep")
     partners = others("rep", reps)
     greet(partners)
     copies = []
@@ -371,69 +518,71 @@
         )
         copy.start()
         copies.append(copy)
-    total = sums[...]
-    for d, copy in enumerate(copies):
+    for copy in copies:
         copy.wait_recv()
-        total = total + landed[d]
-    out[...] = total
+    if last:
+        heights, weighted = (
+            sum((landed[d, k, part] for d in range(reps - 1)), sums[k, part]) for k in range(2)
+        )
+        heights = heights + FLOOR
+        outs[0][...] = -(weighted + UNMATCHED * FLOOR) / heights
+        outs[1][...] = (SHIFT - jnp.log2(heights)) * (1.0 / SCALE)
+    else:
+        total = sum((landed[d, 0] for d in range(reps - 1)), sums[0])
+        outs[0][...] = SHIFT - jnp.log2(total + FLOOR)
     for copy in copies:
         copy.wait_send()
 
 
 def row_totals(reps, sums, call):
+    last = call == ITERS - 1
+    sums = sums.reshape(sums.shape[0], reps, -1, sums.shape[2])
     dma = pltpu.SemaphoreType.DMA((reps - 1,))
     vmem = pl.BlockSpec(memory_space=pltpu.VMEM)
+    shapes = [sums.shape[2:]] * 2 if last else [sums.shape[1:]]
     return pl.pallas_call(
-        functools.partial(row_kernel, reps),
-        out_shape=jax.ShapeDtypeStruct(sums.shape, sums.dtype),
+        functools.partial(row_kernel, reps, last),
+        out_shape=[jax.ShapeDtypeStruct(shape, sums.dtype) for shape in shapes],
         in_specs=[vmem],
-        out_specs=vmem,
+        out_specs=[vmem] * len(shapes),
         scratch_shapes=[pltpu.VMEM((reps - 1,) + sums.shape, jnp.float32), dma, dma],
-        compiler_params=pltpu.CompilerParams(collective_id=3 + call, has_side_effects=True),
+        compiler_params=pltpu.CompilerParams(
+            collective_id=1 + ITERS + call, has_side_effects=True, vmem_limit_bytes=2 * MIB
+        ),
         name="row_exchange_%d" % call,
     )(sums)
 
 
 def body(rollout, demo, projection, location, pair_block, pair_count):
-    own_blocks, slots = pair_block.shape
-    blk = rollout.shape[0] // own_blocks
-    demo_count = demo.shape[0] // blk
+    blk = rollout.shape[0] // pair_block.shape[0]
     n = lax.axis_size("roll")
     reps = lax.axis_size("rep")
-    part = lax.axis_index("rep")
-    share = demo_count // reps
-    own_demo = lax.dynamic_slice_in_dim(demo, part * (share * blk), share * blk, 0)
-    own_v = project(own_demo, projection)
-    own_u = project(rollout, projection)
-    own_pairs = jnp.concatenate([pair_block, pair_count[:, None]], axis=1)
-    own_pairs = jnp.pad(own_pairs, ((0, 0), (0, 128 - own_pairs.shape[1])))
-    own = (own_v, norms(own_v, blk), own_u, norms(own_u, blk), own_pairs)
     if n <= DIRECT:
-        v, vnorm, u, unorm, pairs = gathered(n, reps, *own)
+        v, vnorm, u, unorm, lists = gathered(
+            n, reps, demo, rollout, projection, pair_block, pair_count, location
+        )
     else:
-        v, vnorm = (lax.all_gather(a, "roll") for a in own[:2])
-        u, unorm, pairs = (lax.all_gather(a, "rep") for a in own[2:])
-    v, vnorm, u, unorm, pairs = (a.reshape(-1, a.shape[-1]) for a in (v, vnorm, u, unorm, pairs))
-    lists = listed(pairs[:, :slots], pairs[:, slots], location, demo_count, share, part)
-
-    roll_pot = jnp.zeros_like(unorm)
-    for iteration in range(2):
-        sums = run_pass("column", lists, u, v, unorm, vnorm, roll_pot)
-        demo_pot = column_potentials(n, sums, iteration)
-        kind = "final" if iteration == 1 else "row"
-        sums = run_pass(kind, lists, u, v, unorm, vnorm, demo_pot)
-        sums = row_totals(reps, sums, iteration)
-        heights = sums[0] + FLOOR
-        roll_pot = SHIFT - jnp.log2(heights)
-    reward = -(sums[1] + UNMATCHED * FLOOR) / heights
-    mine = lax.axis_index("roll") * share
-    own_pot = lax.all_gather(lax.dynamic_slice_in_dim(demo_pot, mine, share, 0), "rep", tiled=True)
-    first = part * own_blocks
-    return (
-        lax.dynamic_slice_in_dim(reward, first, own_blocks, 0).reshape(-1),
-        lax.dynamic_slice_in_dim(roll_pot, first, own_blocks, 0).reshape(-1) / SCALE,
-        own_pot.reshape(-1) / SCALE,
-    )
+        part = lax.axis_index("rep")
+        demo_count = demo.shape[0] // blk
+        share = demo_count // reps
+        own_demo = lax.dynamic_slice_in_dim(demo, part * (share * blk), share * blk, 0)
+        own_v = project(own_demo, projection)
+        own_u = project(rollout, projection)
+        v, vnorm = (lax.all_gather(a, "roll") for a in (own_v, norms(own_v, blk)))
+        u, unorm = (lax.all_gather(a, "rep") for a in (own_u, norms(own_u, blk)))
+        pairs, counts = (lax.all_gather(a, "rep", tiled=True) for a in (pair_block, pair_count))
+        lists = listed(pairs, counts, location, demo_count, share, part)
+    v, vnorm, u, unorm = (a.reshape(-1, a.shape[-1]) for a in (v, vnorm, u, unorm))
+
+    roll_pot = unorm
+    for iteration in range(ITERS):
+        sums = run_pass("column", iteration == 0, lists, u, v, unorm, vnorm, roll_pot)
+        demo_pot, held_pot = column_potentials(n, reps, sums, iteration)
+        kind = "final" if iteration == ITERS - 1 else "row"
+        sums = run_pass(kind, False, lists, u, v, unorm, vnorm, demo_pot)
+        results = row_totals(reps, sums, iteration)
+        roll_pot = results[0].reshape(unorm.shape) if kind == "row" else None
+    return results[0].reshape(-1), results[1].reshape(-1), held_pot.reshape(-1)
 
 
 def solution(mesh):

time: 182 us -> 126 us (0.69)
  Pallas kernels: 162 us -> 117 us
  matrix products: 5.75 us -> 0 us
  other arithmetic: 4.55 us -> 0.08 us
  blocking collectives: 4.33 us -> 0 us
  local copies, waits for them, and re-layouts: 5.03 us -> 7.33 us
    pallas_call x9, Pallas kernels: 162 us -> 117 us  [the longest x1 52.2 us: gathered(): pl.pallas_call(functools.partial(gather_kernel, n, reps, slots), out_shap...]
    unnamed x9 -> x12, local copies, waits for them, and re-layouts: 0.09 us -> 6.59 us
    dot_general x2 -> x0, matrix products: 5.75 us -> none  [project(): jnp.dot(frames, projection, preferred_element_type=jnp.float32)]
    all_gather x1 -> x0, blocking collectives: 4.33 us -> none  [body(): lax.all_gather(lax.dynamic_slice_in_dim(demo_pot, mine, share, 0), 'rep',...]
where the time goes in v3:
time: 126 us; the launch traced here: 125 us
  Pallas kernels  117 us (93%)
  local copies, waits for them, and re-layouts  7.33 us (6%)
    pallas_call x1, Pallas kernels, gathered(): pl.pallas_call(functools.partial(gather_kernel, n, reps, slots), out_shap...  52.2 us
    pallas_call x2, Pallas kernels, column_potentials(): pl.pallas_call(functools.partial(column_kernel, n, reps if last else 0),...  30.7 us
    pallas_call x4, Pallas kernels, run_pass(): pl.pallas_call(functools.partial(pass_kernel, kind, first), out_shape=out...  23.5 us
    pallas_call x2, Pallas kernels, row_totals(): pl.pallas_call(functools.partial(row_kernel, reps, last), out_shape=[jax....  10.4 us
    unnamed x12, local copies, waits for them, and re-layouts  6.59 us

profile of v3, /device:TPU:0, one launch (start us, length us, event | category | flops | bytes accessed | tf_op | source)
XLA Modules:
  0.0 124.9 jit_solution(7292428924948039928)
XLA Ops:
  0.6 0.8 copy.9
  1.4 0.7 copy.10
  2.1 0.1 pad_add_fusion
  2.2 0.0 copy-start
  2.2 1.2 copy-done
  3.4 0.0 copy-start.1
  3.4 1.2 copy-done.1
  4.7 0.0 copy-start.2
  4.7 0.9 copy-done.2
  5.6 0.0 copy-start.3
  5.6 0.7 copy-done.3
  6.2 52.2 %gather_codes.1 = (bf16[16,1024,256]{2,1,0:T(8,128)(2,1)S(1)}, f32[16,8,128]{2,1,0:T(8,128)S(1)}, bf16[2,2048,256]{2,1,0:T(8,128)(2,1)S(1)}, f32[2,16,128]{2,1,0:T(8,128)S(1)}, s32[8,384]{1,0:T(8,128)S(1)}) custom-call(bf16[2048,256]{1,0:T(8,128)(2,1)S(1)} %copy-done, bf16[2048,256]{1,0:T(8,128)(2,1)S(1)} %copy-done.1, bf16[256,256]{1,0:T(8,128)(2,1)S(1)} %copy-done.2, ...), custom_call_target="tpu_custom_call" | custom-call | tf_op jit(solution)/shard_map/gather_codes/pallas_call | solution.py:388
  58.4 5.2 %pass_column.2 = f32[128,128]{1,0:T(8,128)S(1)} custom-call(s32[8,384]{1,0:T(8,128)S(1)} %get-tuple-element.12.lists_ref, bf16[4096,256]{1,0:T(8,128)(2,1)S(1)} %bitcast.20, bf16[16384,256]{1,0:T(8,128)(2,1)S(1)} %bitcast.16, f32[32,128]{1,0:T(8,128)S(1)} %bitcast.28, f32[128,128]{1,0:T(8,128)S(1)} %bitcast.24, f32[32,128]{1,0:T(8,128)S(1)} %bitcast.29), custom_call_target="tpu_custom_call" | custom-call | flops 1073741824 | bytes 10485760 | tf_op jit(solution)/shard_map/pass_column/pallas_call | solution.py:124
  63.7 14.2 %column_exchange_0.1 = f32[16,8,128]{2,1,0:T(8,128)S(1)} custom-call(f32[16,8,128]{2,1,0:T(8,128)S(1)} %bitcast.35), custom_call_target="tpu_custom_call" | custom-call | tf_op jit(solution)/shard_map/column_exchange_0/pallas_call | solution.py:494
  77.9 6.1 %pass_row.1 = f32[1,32,128]{2,1,0:T(8,128)S(1)} custom-call(s32[8,384]{1,0:T(8,128)S(1)} %get-tuple-element.12.lists_ref, bf16[4096,256]{1,0:T(8,128)(2,1)S(1)} %bitcast.21, bf16[16384,256]{1,0:T(8,128)(2,1)S(1)} %bitcast.17, f32[32,128]{1,0:T(8,128)S(1)} %bitcast.30, f32[128,128]{1,0:T(8,128)S(1)} %bitcast.25, f32[128,128]{1,0:T(8,128)S(1)} %bitcast.34), custom_call_target="tpu_custom_call" | custom-call | flops 1073741824 | bytes 10485760 | tf_op jit(solution)/shard_map/pass_row/pallas_call | solution.py:124
  84.0 5.1 %row_exchange_0.1 = f32[2,16,128]{2,1,0:T(8,128)S(1)} custom-call(f32[1,2,16,128]{3,2,1,0:T(8,128)S(1)} %bitcast.38), custom_call_target="tpu_custom_call" | custom-call | tf_op jit(solution)/shard_map/row_exchange_0/pallas_call | solution.py:543
  89.1 5.2 %pass_column.3 = f32[128,128]{1,0:T(8,128)S(1)} custom-call(s32[8,384]{1,0:T(8,128)S(1)} %get-tuple-element.12.lists_ref, bf16[4096,256]{1,0:T(8,128)(2,1)S(1)} %bitcast.22, bf16[16384,256]{1,0:T(8,128)(2,1)S(1)} %bitcast.18, f32[32,128]{1,0:T(8,128)S(1)} %bitcast.31, f32[128,128]{1,0:T(8,128)S(1)} %bitcast.26, f32[32,128]{1,0:T(8,128)S(1)} %bitcast.39), custom_call_target="tpu_custom_call" | custom-call | flops 1073741824 | bytes 10485760 | tf_op jit(solution)/shard_map/pass_column/pallas_call | solution.py:124
  94.3 16.5 %column_exchange_1.1 = (f32[16,8,128]{2,1,0:T(8,128)S(1)}, f32[2,8,128]{2,1,0:T(8,128)S(1)}) custom-call(f32[16,8,128]{2,1,0:T(8,128)S(1)} %bitcast.33), custom_call_target="tpu_custom_call" | custom-call | tf_op jit(solution)/shard_map/column_exchange_1/pallas_call | solution.py:494
  110.8 6.9 %pass_final.1 = f32[2,32,128]{2,1,0:T(8,128)S(1)} custom-call(s32[8,384]{1,0:T(8,128)S(1)} %get-tuple-element.12.lists_ref, bf16[4096,256]{1,0:T(8,128)(2,1)S(1)} %bitcast.23, bf16[16384,256]{1,0:T(8,128)(2,1)S(1)} %bitcast.19, f32[32,128]{1,0:T(8,128)S(1)} %bitcast.32, f32[128,128]{1,0:T(8,128)S(1)} %bitcast.27, f32[128,128]{1,0:T(8,128)S(1)} %bitcast.37), custom_call_target="tpu_custom_call" | custom-call | flops 1073741824 | bytes 10485760 | tf_op jit(solution)/shard_map/pass_final/pallas_call | solution.py:124
  117.7 5.3 %row_exchange_1.1 = (f32[16,128]{1,0:T(8,128)S(1)}, f32[16,128]{1,0:T(8,128)S(1)}) custom-call(f32[2,2,16,128]{3,2,1,0:T(8,128)S(1)} %bitcast.36), custom_call_target="tpu_custom_call" | custom-call | tf_op jit(solution)/shard_map/row_exchange_1/pallas_call | solution.py:543
  123.1 0.6 copy.14
  123.7 0.6 copy.15
  124.3 0.6 copy.16
  (1 shorter events, 0.0 us)
Async XLA Ops:
  2.2 1.2 copy-start
  3.4 1.2 copy-start.1
  4.7 0.9 copy-start.2
  5.6 0.7 copy-start.3

commit v4 on v3

--- a/solution.py
+++ b/solution.py
@@ -22,31 +22,46 @@
 MESH = pl.DeviceIdType.MESH
 
 
-def pass_kernel(kind, first, lists_ref, u_ref, v_ref, unorm_ref, vnorm_ref, pot_ref, *rest):
-    roll_blocks, blk = unorm_ref.shape
-    feats = u_ref.shape[1]
-    unit = SCALE / feats
-    if kind == "column":
-        out_ref, row_term, col_acc = rest
-        col_acc[...] = jnp.zeros_like(col_acc)
-    elif kind == "row":
-        out_ref, row_term, col_term, acc = rest
-        acc[...] = jnp.zeros_like(acc)
+def pass_kernel(kind, fresh, stored, lists_ref, *refs):
+    refs = list(refs)
+    reads = stored and not fresh
+    if reads:
+        kept = refs.pop(0)
     else:
-        out_ref, row_term, col_term, acc, wacc = rest
-        acc[...] = jnp.zeros_like(acc)
-        wacc[...] = jnp.zeros_like(wacc)
-
-    def prepare(b, carry):
-        line = unorm_ref[pl.ds(b, 1), :] * (-unit)
-        if kind == "column":
-            line = line + (SHIFT if first else pot_ref[pl.ds(b, 1), :] + SHIFT)
-        row_term[pl.ds(b * blk, blk), :] = jnp.transpose(jnp.broadcast_to(line, (blk, blk)))
-        return carry
-
-    lax.fori_loop(0, roll_blocks, prepare, 0, unroll=8)
-    if kind != "column":
-        col_term[...] = pot_ref[...] + SHIFT
+        u_ref, v_ref, unorm_ref, vnorm_ref = refs[:4]
+        refs = refs[4:]
+    pot_ref = None if fresh else refs.pop(0)
+    out_ref = refs.pop(0)
+    if stored and fresh:
+        kept = refs.pop(0)
+    sums_ref = refs.pop()
+    if kind == "final":
+        wsums_ref = refs.pop()
+        wsums_ref[...] = jnp.zeros_like(wsums_ref)
+    sums_ref[...] = jnp.zeros_like(sums_ref)
+    blk = out_ref.shape[-1]
+    by_column = kind == "column"
+    roll_blocks = (refs[0] if refs else sums_ref).shape[0] // blk
+
+    if not reads:
+        row_norm = refs.pop(0)
+        unit = SCALE / u_ref.shape[1]
+        roll_blocks = unorm_ref.shape[0]
+
+    def spread(source, factor, target):
+        def one(b, carry):
+            line = source[pl.ds(b, 1), :] * factor
+            rows = pl.ds(pl.multiple_of(b * blk, blk), blk)
+            target[rows, :] = jnp.transpose(jnp.broadcast_to(line, (blk, blk)))
+            return carry
+
+        lax.fori_loop(0, roll_blocks, one, 0, unroll=8)
+
+    if not reads:
+        spread(unorm_ref, -unit, row_norm)
+    if by_column and not fresh:
+        row_pot = refs.pop(0)
+        spread(pot_ref, 1.0, row_pot)
 
     total = lists_ref[2, 0]
 
@@ -56,85 +71,92 @@
             at = k * UNROLL + p
             b = lists_ref[0, at]
             t = lists_ref[1, at]
-            live = jnp.where(at < total, 0.0, -1e30)
+            live = jnp.where(at < total, SHIFT, -1e30)
             rows = pl.ds(pl.multiple_of(b * blk, blk), blk)
-            crossed = lax.dot_general(
-                u_ref[rows, :],
-                v_ref[pl.ds(pl.multiple_of(t * blk, blk), blk), :],
-                (((1,), (1,)), ((), ())),
-                preferred_element_type=jnp.float32,
-            )
-            y = crossed * (2.0 * unit) + row_term[rows, :]
-            line = vnorm_ref[pl.ds(t, 1), :] * (-unit)
-            if kind == "column":
-                e = jnp.exp2(y + (line + live))
-                parts.append((t, jnp.sum(e.reshape(blk // 8, 8, blk), axis=0)))
-            elif kind == "row":
-                e = jnp.exp2(y + (line + (col_term[pl.ds(t, 1), :] + live)))
-                parts.append((rows, e))
+            here = pl.ds(pl.multiple_of(at * blk, blk), blk)
+            if reads:
+                y = kept[here, :]
             else:
-                y = y + line
-                e = jnp.exp2(y + (col_term[pl.ds(t, 1), :] + live))
-                parts.append((rows, e, e * y))
-        for part in parts:
-            if kind == "column":
-                at8 = pl.ds(pl.multiple_of(part[0] * 8, 8), 8)
-                col_acc[at8, :] = col_acc[at8, :] + part[1]
+                crossed = lax.dot_general(
+                    u_ref[rows, :],
+                    v_ref[pl.ds(pl.multiple_of(t * blk, blk), blk), :],
+                    (((1,), (1,)), ((), ())),
+                    preferred_element_type=jnp.float32,
+                )
+                y = crossed * (2.0 * unit) + row_norm[rows, :] + vnorm_ref[pl.ds(t, 1), :] * (-unit)
+                if stored:
+                    kept[here, :] = y
+            if by_column:
+                x = y + live if fresh else y + row_pot[rows, :] + live
+                parts.append((t, jnp.sum(jnp.exp2(x).reshape(blk // 8, 8, blk), axis=0)))
             else:
-                acc[part[0], :] = acc[part[0], :] + part[1]
+                e = jnp.exp2(y + (pot_ref[pl.ds(t, 1), :] + live))
+                parts.append((rows, e, e * y if kind == "final" else None))
+        for where, e, *weighted in parts:
+            if by_column:
+                at8 = pl.ds(pl.multiple_of(where * 8, 8), 8)
+                sums_ref[at8, :] = sums_ref[at8, :] + e
+            else:
+                sums_ref[where, :] = sums_ref[where, :] + e
                 if kind == "final":
-                    wacc[part[0], :] = wacc[part[0], :] + part[2]
+                    wsums_ref[where, :] = wsums_ref[where, :] + weighted[0]
         return carry
 
     lax.fori_loop(0, (total + UNROLL - 1) // UNROLL, step, 0)
 
-    if kind == "column":
-        targets = out_ref.shape[0]
-        out_ref[...] = jnp.sum(col_acc[...].reshape(targets, 8, blk), axis=1)
+    if by_column:
+        out_ref[...] = jnp.sum(sums_ref[...].reshape(out_ref.shape[0], 8, blk), axis=1)
     else:
 
         def finish(b, carry):
             rows = pl.ds(pl.multiple_of(b * blk, blk), blk)
-            out_ref[0, pl.ds(b, 1), :] = jnp.sum(jnp.transpose(acc[rows, :]), axis=0, keepdims=True)
+            out_ref[0, pl.ds(b, 1), :] = jnp.sum(jnp.transpose(sums_ref[rows, :]), axis=0, keepdims=True)
             if kind == "final":
                 out_ref[1, pl.ds(b, 1), :] = jnp.sum(
-                    jnp.transpose(wacc[rows, :]), axis=0, keepdims=True
+                    jnp.transpose(wsums_ref[rows, :]), axis=0, keepdims=True
                 ) * (-1.0 / SCALE)
             return carry
 
         lax.fori_loop(0, roll_blocks, finish, 0, unroll=8)
 
 
-def run_pass(kind, first, lists, u, v, unorm, vnorm, pot):
+def run_pass(kind, lists, u, v, unorm, vnorm, pot, kept, stored):
+    fresh = pot is None
     roll_blocks, blk = unorm.shape
     targets = vnorm.shape[0]
+    pairs = lists.shape[1] - 128
     smem = pl.BlockSpec(memory_space=pltpu.SMEM)
     vmem = pl.BlockSpec(memory_space=pltpu.VMEM)
     frames = pltpu.VMEM((roll_blocks * blk, blk), jnp.float32)
-    if kind == "column":
-        out = jax.ShapeDtypeStruct((targets, blk), jnp.float32)
-        scratch = [frames, pltpu.VMEM((targets * 8, blk), jnp.float32)]
+    by_column = kind == "column"
+    reads = stored and not fresh
+    args = [kept] if reads else [u, v, unorm, vnorm]
+    if not fresh:
+        args.append(pot)
+    if by_column:
+        outs = [jax.ShapeDtypeStruct((targets, blk), jnp.float32)]
+        sums = [pltpu.VMEM((targets * 8, blk), jnp.float32)]
     else:
-        out = jax.ShapeDtypeStruct((2 if kind == "final" else 1, roll_blocks, blk), jnp.float32)
-        scratch = [frames, pltpu.VMEM((targets, blk), jnp.float32), frames]
-        if kind == "final":
-            scratch.append(frames)
-    pairs = lists.shape[1] // 3
-    held = sum(math.prod(a.shape) * a.dtype.itemsize for a in [u, v, out] + scratch)
+        outs = [jax.ShapeDtypeStruct((2 if kind == "final" else 1, roll_blocks, blk), jnp.float32)]
+        sums = [frames] * (2 if kind == "final" else 1)
+    if stored and fresh:
+        outs.append(jax.ShapeDtypeStruct(((pairs + UNROLL) * blk, blk), jnp.float32))
+    scratch = ([] if reads else [frames]) + ([frames] if by_column and not fresh else []) + sums
+    held = sum(math.prod(a.shape) * a.dtype.itemsize for a in scratch + ([] if stored else args + outs))
     return pl.pallas_call(
-        functools.partial(pass_kernel, kind, first),
-        out_shape=out,
-        in_specs=[smem] + [vmem] * 5,
-        out_specs=vmem,
+        functools.partial(pass_kernel, kind, fresh, stored),
+        out_shape=outs,
+        in_specs=[smem] + [vmem] * len(args),
+        out_specs=[vmem] * len(outs),
         scratch_shapes=scratch,
-        compiler_params=pltpu.CompilerParams(vmem_limit_bytes=held + 3 * MIB),
+        compiler_params=pltpu.CompilerParams(vmem_limit_bytes=held + 2 * MIB),
         cost_estimate=pl.CostEstimate(
-            flops=2 * pairs * blk * blk * u.shape[1],
-            bytes_accessed=2 * (u.size + v.size),
-            transcendentals=pairs * blk * blk,
+            flops=0 if reads else pairs * blk * blk * u.shape[1],
+            bytes_accessed=2 * v.size,
+            transcendentals=pairs * blk * blk // 2,
         ),
         name="pass_" + kind,
-    )(lists, u, v, unorm, vnorm, pot)
+    )(lists, *args)
 
 
 def listed(pair_block, pair_count, location, demo_count, share, part):
@@ -193,15 +215,18 @@
 
 def packed_pairs(pairs, location, slots, demo_count, share, part, width):
     blocks = pairs.shape[0]
-    names = lax.broadcasted_iota(jnp.int32, (blocks, location.shape[1]), 1)
+    names = lax.broadcasted_iota(jnp.int32, (blocks, 128), 1).astype(jnp.float32)
     places = lax.broadcasted_iota(jnp.int32, (blocks, width), 1).astype(jnp.float32)
     number = lax.broadcasted_iota(jnp.int32, (blocks, width), 0).astype(jnp.float32)
     count = pairs[:, slots : slots + 1]
     where_held = location.astype(jnp.float32)
     mine, target = [], []
     for s in range(slots):
-        hit = pairs[:, s : s + 1] == names
-        stored = jnp.sum(jnp.where(hit, where_held, 0.0), axis=1, keepdims=True)
+        found = jnp.zeros((blocks, 128), jnp.float32)
+        for k in range(location.shape[0]):
+            hit = pairs[:, s : s + 1] - 128.0 * k == names
+            found = found + jnp.where(hit, where_held[k : k + 1, :], 0.0)
+        stored = jnp.sum(found, axis=1, keepdims=True)
         owner = jnp.floor((stored + 0.5) * (1.0 / demo_count))
         local = stored - owner * demo_count
         side = jnp.floor((local + 0.5) * (1.0 / share))
@@ -225,10 +250,10 @@
 
 
 def gather_kernel(n, reps, slots, *refs):
-    demo, rollout, projection, own_pairs, location = refs[:5]
-    v, vnorm, u, unorm, lists = refs[5:10]
-    (demo_in, rollout_in, own_v, own_vnorm, own_u, own_unorm, pairs,
-     ring_send, ring_recv, side_send, side_recv, norm_send, norm_recv, rep_send, rep_recv, home) = refs[10:]
+    demo, rollout, projection_hbm, pair_block, pair_count, location_hbm = refs[:6]
+    v, vnorm, u, unorm, lists = refs[6:11]
+    (demo_in, rollout_in, projection, location, block_in, count_in, own_pairs, own_v, own_vnorm, own_u, own_unorm, pairs,
+     ring_send, ring_recv, side_send, side_recv, norm_send, norm_recv, rep_send, rep_recv, home) = refs[11:]
     me = lax.axis_index("roll")
     part = lax.axis_index("rep")
     chips = n // 2
@@ -251,12 +276,28 @@
     near = others("roll", n) + others("rep", reps)
     fetch_demo = pltpu.make_async_copy(demo.at[pl.ds(part * (share * blk), share * blk)], demo_in, home.at[4])
     fetch_demo.start()
+    fetches = [
+        pltpu.make_async_copy(source, target, home.at[6 + k])
+        for k, (source, target) in enumerate((
+            (projection_hbm, projection),
+            (pair_block, block_in),
+            (pair_count, count_in),
+            (location_hbm, location),
+        ))
+    ]
+    for fetch in fetches:
+        fetch.start()
     fetch_rollout = pltpu.make_async_copy(rollout, rollout_in, home.at[5])
     fetch_rollout.start()
     barrier = pltpu.get_barrier_semaphore()
     for partner in near:
         pl.semaphore_signal(barrier, inc=1, device_id=partner, device_id_type=MESH)
     fetch_demo.wait()
+    for fetch in fetches:
+        fetch.wait()
+    own_pairs[...] = jnp.zeros_like(own_pairs)
+    own_pairs[0:slots, 0 : block_in.shape[1]] = block_in[...]
+    own_pairs[slots : slots + 1, 0 : count_in.shape[1]] = count_in[...]
     for half in range(2):
         piece = pl.ds(half * rows, rows)
         own_v[piece, :] = jnp.dot(
@@ -351,7 +392,11 @@
         stays.append(copy)
     for copy in pair_copies:
         copy.wait()
-    everyone = pairs[...].reshape(reps * own_blocks, pairs.shape[2])
+    square = [
+        jnp.concatenate([pairs[r].astype(jnp.float32), jnp.zeros((128 - pairs.shape[1], 128), jnp.float32)], axis=0)
+        for r in range(reps)
+    ]
+    everyone = jnp.concatenate([jnp.transpose(a)[0:own_blocks, :] for a in square], axis=0)
     found = packed_pairs(everyone, location[...], slots, share * reps, share, part, lists.shape[1])
     lists[...] = jnp.zeros_like(lists)
     for k, row in enumerate(found):
@@ -379,8 +424,9 @@
     blk = rollout.shape[0] // own_blocks
     feats = projection.shape[1]
     share = demo.shape[0] // blk // reps
-    own_pairs = jnp.concatenate([pair_block, pair_count[:, None]], axis=1)
-    own_pairs = jnp.pad(own_pairs, ((0, 0), (0, 128 - own_pairs.shape[1])))
+    location = location.reshape(-1, 128)
+    own_pairs = (slots // 8 * 8 + 8, 128)
+    hbm = pl.BlockSpec(memory_space=pltpu.HBM)
     anywhere = pl.BlockSpec(memory_space=pl.ANY)
     vmem = pl.BlockSpec(memory_space=pltpu.VMEM)
     dma = pltpu.SemaphoreType.DMA
@@ -394,27 +440,35 @@
             jax.ShapeDtypeStruct((reps, own_blocks, blk), wide),
             jax.ShapeDtypeStruct((8, reps * own_blocks * slots + 128), jnp.int32),
         ],
-        in_specs=[anywhere, anywhere, vmem, vmem, vmem],
+        in_specs=[hbm] * 6,
         out_specs=[anywhere] * 4 + [vmem],
         scratch_shapes=[
             pltpu.VMEM((share * blk, feats), code),
             pltpu.VMEM(rollout.shape, code),
+            pltpu.VMEM(projection.shape, code),
+            pltpu.VMEM(location.shape, jnp.int32),
+            pltpu.VMEM((slots, own_blocks), jnp.int32),
+            pltpu.VMEM((1, own_blocks), jnp.int32),
+            pltpu.VMEM(own_pairs, jnp.int32),
             pltpu.VMEM((share * blk, feats), code),
             pltpu.VMEM((share, blk), wide),
             pltpu.VMEM((own_blocks * blk, feats), code),
             pltpu.VMEM((own_blocks, blk), wide),
-            pltpu.VMEM((reps,) + own_pairs.shape, jnp.int32),
+            pltpu.VMEM((reps,) + own_pairs, jnp.int32),
             dma((2, hops, 2)), dma((2, hops, 2)),
             dma((2, hops + 1, 2)), dma((2, hops + 1, 2)),
             dma((1, n - 1)), dma((1, n - 1)),
             dma((3, reps - 1)), dma((3, reps - 1)),
-            dma((6,)),
+            dma((10,)),
         ],
         compiler_params=pltpu.CompilerParams(
             collective_id=0, has_side_effects=True, vmem_limit_bytes=8 * MIB
         ),
         name="gather_codes",
-    )(demo, rollout, projection, own_pairs, location[None, :])
+    )(*(
+        pltpu.with_memory_space_constraint(a, pltpu.HBM)
+        for a in (demo, rollout, projection, pair_block.T, pair_count[None, :], location)
+    ))
 
 
 def column_kernel(n, reps, sums, *refs):
@@ -574,12 +628,14 @@
         lists = listed(pairs, counts, location, demo_count, share, part)
     v, vnorm, u, unorm = (a.reshape(-1, a.shape[-1]) for a in (v, vnorm, u, unorm))
 
-    roll_pot = unorm
+    stored = n <= DIRECT
+    roll_pot = kept = None
     for iteration in range(ITERS):
-        sums = run_pass("column", iteration == 0, lists, u, v, unorm, vnorm, roll_pot)
+        sums, *rest = run_pass("column", lists, u, v, unorm, vnorm, roll_pot, kept, stored)
+        kept = rest[0] if rest else kept
         demo_pot, held_pot = column_potentials(n, reps, sums, iteration)
         kind = "final" if iteration == ITERS - 1 else "row"
-        sums = run_pass(kind, False, lists, u, v, unorm, vnorm, demo_pot)
+        sums = run_pass(kind, lists, u, v, unorm, vnorm, demo_pot, kept, stored)[0]
         results = row_totals(reps, sums, iteration)
         roll_pot = results[0].reshape(unorm.shape) if kind == "row" else None
     return results[0].reshape(-1), results[1].reshape(-1), held_pot.reshape(-1)

time: 126 us -> 103 us (0.82)
  Pallas kernels: 117 us -> 99.9 us
  local copies, waits for them, and re-layouts: 7.33 us -> 1.8 us
    pallas_call x4, Pallas kernels: 23.5 us -> 14.5 us  [run_pass(): pl.pallas_call(functools.partial(pass_kernel, kind, fresh, stored), out_s...]
    pallas_call x2, Pallas kernels: 30.7 us -> 25.4 us  [column_potentials(): pl.pallas_call(functools.partial(column_kernel, n, reps if last else 0),...]
    unnamed x12 -> x3, local copies, waits for them, and re-layouts: 6.59 us -> 1.8 us
    pallas_call x2, Pallas kernels: 10.4 us -> 7.79 us  [row_totals(): pl.pallas_call(functools.partial(row_kernel, reps, last), out_shape=[jax....]
where the time goes in v4:
time: 103 us; the launch traced here: 102 us
  Pallas kernels  99.9 us (97%)
  local copies, waits for them, and re-layouts  1.8 us (2%)
    pallas_call x1, Pallas kernels, gathered(): pl.pallas_call(functools.partial(gather_kernel, n, reps, slots), out_shap...  52.2 us
    pallas_call x2, Pallas kernels, column_potentials(): pl.pallas_call(functools.partial(column_kernel, n, reps if last else 0),...  25.4 us
    pallas_call x4, Pallas kernels, run_pass(): pl.pallas_call(functools.partial(pass_kernel, kind, fresh, stored), out_s...  14.5 us
    pallas_call x2, Pallas kernels, row_totals(): pl.pallas_call(functools.partial(row_kernel, reps, last), out_shape=[jax....  7.79 us

profile of v4, /device:TPU:0, one launch (start us, length us, event | category | flops | bytes accessed | tf_op | source)
XLA Modules:
  0.0 102.4 jit_solution(9220839845852711799)
XLA Ops:
  0.6 52.2 %gather_codes.1 = (bf16[16,1024,256]{2,1,0:T(8,128)(2,1)S(1)}, f32[16,8,128]{2,1,0:T(8,128)S(1)}, bf16[2,2048,256]{2,1,0:T(8,128)(2,1)S(1)}, f32[2,16,128]{2,1,0:T(8,128)S(1)}, s32[8,384]{1,0:T(8,128)S(1)}) custom-call(bf16[2048,256]{1,0:T(8,128)(2,1)} %refs_0_.1, bf16[2048,256]{1,0:T(8,128)(2,1)} %refs_1_.1, bf16[256,256]{1,0:T(8,128)(2,1)} %refs_2_.1, ...), custom_call_target="tpu_custom_call" | custom-call | tf_op jit(solution)/shard_map/gather_codes/pallas_call | solution.py:434
  52.9 5.7 %pass_column.2 = (f32[128,128]{1,0:T(8,128)S(1)}, f32[33280,128]{1,0:T(8,128)S(1)}) custom-call(s32[8,384]{1,0:T(8,128)S(1)} %get-tuple-element.14.lists_ref, bf16[4096,256]{1,0:T(8,128)(2,1)S(1)} %bitcast.18, bf16[16384,256]{1,0:T(8,128)(2,1)S(1)} %bitcast.17, f32[32,128]{1,0:T(8,128)S(1)} %bitcast.27, f32[128,128]{1,0:T(8,128)S(1)} %bitcast.22), custom_call_target="tpu_custom_call" | custom-call | flops 1073741824 | bytes 8388608 | tf_op jit(solution)/shard_map/pass_column/pallas_call | solution.py:146
  58.6 13.7 %column_exchange_0.1 = f32[16,8,128]{2,1,0:T(8,128)S(1)} custom-call(f32[16,8,128]{2,1,0:T(8,128)S(1)} %bitcast.26), custom_call_target="tpu_custom_call" | custom-call | tf_op jit(solution)/shard_map/column_exchange_0/pallas_call | solution.py:548
  72.3 2.6 %pass_row.1 = f32[1,32,128]{2,1,0:T(8,128)S(1)} custom-call(s32[8,384]{1,0:T(8,128)S(1)} %get-tuple-element.14.lists_ref, f32[33280,128]{1,0:T(8,128)S(1)} %get-tuple-element.19.refs_0_, f32[128,128]{1,0:T(8,128)S(1)} %bitcast.20), custom_call_target="tpu_custom_call" | custom-call | bytes 8388608 | tf_op jit(solution)/shard_map/pass_row/pallas_call | solution.py:146
  74.9 3.8 %row_exchange_0.1 = f32[2,16,128]{2,1,0:T(8,128)S(1)} custom-call(f32[1,2,16,128]{3,2,1,0:T(8,128)S(1)} %bitcast.24), custom_call_target="tpu_custom_call" | custom-call | tf_op jit(solution)/shard_map/row_exchange_0/pallas_call | solution.py:597
  78.7 2.7 %pass_column.3 = f32[128,128]{1,0:T(8,128)S(1)} custom-call(s32[8,384]{1,0:T(8,128)S(1)} %get-tuple-element.14.lists_ref, f32[33280,128]{1,0:T(8,128)S(1)} %get-tuple-element.19.refs_0_, f32[32,128]{1,0:T(8,128)S(1)} %bitcast.25), custom_call_target="tpu_custom_call" | custom-call | bytes 8388608 | tf_op jit(solution)/shard_map/pass_column/pallas_call | solution.py:146
  81.3 11.7 %column_exchange_1.1 = (f32[16,8,128]{2,1,0:T(8,128)S(1)}, f32[2,8,128]{2,1,0:T(8,128)S(1)}) custom-call(f32[16,8,128]{2,1,0:T(8,128)S(1)} %bitcast.19), custom_call_target="tpu_custom_call" | custom-call | tf_op jit(solution)/shard_map/column_exchange_1/pallas_call | solution.py:548
  93.0 3.5 %pass_final.1 = f32[2,32,128]{2,1,0:T(8,128)S(1)} custom-call(s32[8,384]{1,0:T(8,128)S(1)} %get-tuple-element.14.lists_ref, f32[33280,128]{1,0:T(8,128)S(1)} %get-tuple-element.19.refs_0_, f32[128,128]{1,0:T(8,128)S(1)} %bitcast.23), custom_call_target="tpu_custom_call" | custom-call | bytes 8388608 | tf_op jit(solution)/shard_map/pass_final/pallas_call | solution.py:146
  96.6 4.0 %row_exchange_1.1 = (f32[16,128]{1,0:T(8,128)S(1)}, f32[16,128]{1,0:T(8,128)S(1)}) custom-call(f32[2,2,16,128]{3,2,1,0:T(8,128)S(1)} %bitcast.21), custom_call_target="tpu_custom_call" | custom-call | tf_op jit(solution)/shard_map/row_exchange_1/pallas_call | solution.py:597
  100.6 0.6 copy.12
  101.2 0.6 copy.13
  101.8 0.6 copy.14

commit v5 on v4

--- a/solution.py
+++ b/solution.py
@@ -18,6 +18,7 @@
 FLOOR = math.exp(SLACK + 50.0)
 UNROLL = 4
 DIRECT = 16
+CHUNKS = 4
 MIB = 1024 * 1024
 MESH = pl.DeviceIdType.MESH
 
@@ -45,7 +46,8 @@
 
     if not reads:
         row_norm = refs.pop(0)
-        unit = SCALE / u_ref.shape[1]
+        feats = u_ref.shape[1]
+        unit = SCALE / feats
         roll_blocks = unorm_ref.shape[0]
 
     def spread(source, factor, target):
@@ -79,8 +81,8 @@
             else:
                 crossed = lax.dot_general(
                     u_ref[rows, :],
-                    v_ref[pl.ds(pl.multiple_of(t * blk, blk), blk), :],
-                    (((1,), (1,)), ((), ())),
+                    v_ref[pl.ds(pl.multiple_of(t * feats, feats), feats), :],
+                    (((1,), (0,)), ((), ())),
                     preferred_element_type=jnp.float32,
                 )
                 y = crossed * (2.0 * unit) + row_norm[rows, :] + vnorm_ref[pl.ds(t, 1), :] * (-unit)
@@ -270,7 +272,8 @@
 
     twin = {"roll": me + 1 - 2 * core}
     ways = ({"roll": at_place(place + 1)}, {"roll": at_place(place - 1)})
-    rows = own_v.shape[0] // 2
+    rows = own_v.shape[0] // CHUNKS
+    feats = projection.shape[1]
     share, blk = own_vnorm.shape
     own_blocks = own_unorm.shape[0]
     near = others("roll", n) + others("rep", reps)
@@ -298,10 +301,11 @@
     own_pairs[...] = jnp.zeros_like(own_pairs)
     own_pairs[0:slots, 0 : block_in.shape[1]] = block_in[...]
     own_pairs[slots : slots + 1, 0 : count_in.shape[1]] = count_in[...]
-    for half in range(2):
-        piece = pl.ds(half * rows, rows)
-        own_v[piece, :] = jnp.dot(
-            demo_in[piece, :], projection[...], preferred_element_type=jnp.float32
+    turned = jnp.transpose(projection[...])
+    for b in range(share):
+        own_v[b * feats : (b + 1) * feats, :] = lax.dot_general(
+            turned, demo_in[b * blk : (b + 1) * blk, :], (((1,), (1,)), ((), ())),
+            preferred_element_type=jnp.float32,
         ).astype(jnp.bfloat16)
     pl.semaphore_wait(barrier, len(near))
 
@@ -338,10 +342,10 @@
         waits.append(copy)
 
     def travels(s, way, half):
-        return s < hops - 1 or (s == hops - 1 and half == way)
+        return s < hops - 1 or (s == hops - 1 and half * 2 // CHUNKS == way)
 
     moving = {}
-    for half in range(2):
+    for half in range(CHUNKS):
         for way in range(2):
             if travels(0, way, half):
                 moving[0, way, half] = send(0, way, half)
@@ -360,7 +364,7 @@
 
     pair_copies = spread(own_pairs, pairs.at[part], "rep", 0, rep_send, rep_recv)
     pairs[part] = own_pairs[...]
-    for half in range(2):
+    for half in range(CHUNKS):
         cross(0, 0, half)
     fetch_rollout.wait()
 
@@ -374,11 +378,17 @@
         return carry
 
     lax.fori_loop(0, own_blocks, do_rollout, 0)
-    waits += spread(own_u, u.at[part], "rep", 1, rep_send, rep_recv)
-    waits += spread(own_unorm, unorm.at[part], "rep", 2, rep_send, rep_recv)
+
+    def send_rollout(q):
+        piece = pl.ds(q * (own_u.shape[0] // hops), own_u.shape[0] // hops)
+        return spread(own_u.at[piece], u.at[part, piece], "rep", 2 + q, rep_send, rep_recv)
+
+    waits += send_rollout(0)
+    waits += spread(own_unorm, unorm.at[part], "rep", 1, rep_send, rep_recv)
 
     def do_demo(b, carry):
-        own_vnorm[pl.ds(b, 1), :] = block_norms(own_v[pl.ds(pl.multiple_of(b * blk, blk), blk), :])
+        wide = own_v[pl.ds(pl.multiple_of(b * feats, feats), feats), :].astype(jnp.float32)
+        own_vnorm[pl.ds(b, 1), :] = jnp.sum(wide * wide, axis=0, keepdims=True)
         return carry
 
     lax.fori_loop(0, share, do_demo, 0)
@@ -402,7 +412,7 @@
     for k, row in enumerate(found):
         lists[k : k + 1, :] = row
     for s in range(1, hops + 1):
-        for half in range(2):
+        for half in range(CHUNKS):
             for way in range(2):
                 if (s - 1, way, half) not in moving:
                     continue
@@ -410,6 +420,8 @@
                 if travels(s, way, half):
                     moving[s, way, half] = send(s, way, half)
                 cross(s, way, half)
+        if s < hops:
+            waits += send_rollout(s)
     for copy in moving.values():
         copy.wait_send()
     for copy in stays:
@@ -434,7 +446,7 @@
     return pl.pallas_call(
         functools.partial(gather_kernel, n, reps, slots),
         out_shape=[
-            jax.ShapeDtypeStruct((n, share * blk, feats), code),
+            jax.ShapeDtypeStruct((n, share * feats, blk), code),
             jax.ShapeDtypeStruct((n, share, blk), wide),
             jax.ShapeDtypeStruct((reps, own_blocks * blk, feats), code),
             jax.ShapeDtypeStruct((reps, own_blocks, blk), wide),
@@ -450,15 +462,15 @@
             pltpu.VMEM((slots, own_blocks), jnp.int32),
             pltpu.VMEM((1, own_blocks), jnp.int32),
             pltpu.VMEM(own_pairs, jnp.int32),
-            pltpu.VMEM((share * blk, feats), code),
+            pltpu.VMEM((share * feats, blk), code),
             pltpu.VMEM((share, blk), wide),
             pltpu.VMEM((own_blocks * blk, feats), code),
             pltpu.VMEM((own_blocks, blk), wide),
             pltpu.VMEM((reps,) + own_pairs, jnp.int32),
-            dma((2, hops, 2)), dma((2, hops, 2)),
-            dma((2, hops + 1, 2)), dma((2, hops + 1, 2)),
+            dma((2, hops, CHUNKS)), dma((2, hops, CHUNKS)),
+            dma((2, hops + 1, CHUNKS)), dma((2, hops + 1, CHUNKS)),
             dma((1, n - 1)), dma((1, n - 1)),
-            dma((3, reps - 1)), dma((3, reps - 1)),
+            dma((2 + hops, reps - 1)), dma((2 + hops, reps - 1)),
             dma((10,)),
         ],
         compiler_params=pltpu.CompilerParams(
@@ -622,7 +634,8 @@
         own_demo = lax.dynamic_slice_in_dim(demo, part * (share * blk), share * blk, 0)
         own_v = project(own_demo, projection)
         own_u = project(rollout, projection)
-        v, vnorm = (lax.all_gather(a, "roll") for a in (own_v, norms(own_v, blk)))
+        flipped = own_v.reshape(share, blk, -1).transpose(0, 2, 1).reshape(-1, blk)
+        v, vnorm = (lax.all_gather(a, "roll") for a in (flipped, norms(own_v, blk)))
         u, unorm = (lax.all_gather(a, "rep") for a in (own_u, norms(own_u, blk)))
         pairs, counts = (lax.all_gather(a, "rep", tiled=True) for a in (pair_block, pair_count))
         lists = listed(pairs, counts, location, demo_count, share, part)

time: 103 us -> 103 us (level)
    pallas_call x4, Pallas kernels: 14.5 us -> 16.4 us  [run_pass(): pl.pallas_call(functools.partial(pass_kernel, kind, fresh, stored), out_s...]
    pallas_call x2, Pallas kernels: 25.4 us -> 24 us  [column_potentials(): pl.pallas_call(functools.partial(column_kernel, n, reps if last else 0),...]
where the time goes in v5:
time: 103 us
  Pallas kernels  100 us (97%)
  local copies, waits for them, and re-layouts  1.8 us (2%)
    pallas_call x1, Pallas kernels, gathered(): pl.pallas_call(functools.partial(gather_kernel, n, reps, slots), out_shap...  51.8 us
    pallas_call x2, Pallas kernels, column_potentials(): pl.pallas_call(functools.partial(column_kernel, n, reps if last else 0),...  24 us
    pallas_call x4, Pallas kernels, run_pass(): pl.pallas_call(functools.partial(pass_kernel, kind, fresh, stored), out_s...  16.4 us
    pallas_call x2, Pallas kernels, row_totals(): pl.pallas_call(functools.partial(row_kernel, reps, last), out_shape=[jax....  8.14 us

profile of v5, /device:TPU:0, one launch (start us, length us, event | category | flops | bytes accessed | tf_op | source)
XLA Modules:
  0.0 102.8 jit_solution(16055754007196662604)
XLA Ops:
  0.6 51.8 %gather_codes.1 = (bf16[16,2048,128]{2,1,0:T(8,128)(2,1)S(1)}, f32[16,8,128]{2,1,0:T(8,128)S(1)}, bf16[2,2048,256]{2,1,0:T(8,128)(2,1)S(1)}, f32[2,16,128]{2,1,0:T(8,128)S(1)}, s32[8,384]{1,0:T(8,128)S(1)}) custom-call(bf16[2048,256]{1,0:T(8,128)(2,1)} %refs_0_.1, bf16[2048,256]{1,0:T(8,128)(2,1)} %refs_1_.1, bf16[256,256]{1,0:T(8,128)(2,1)} %refs_2_.1, ...), custom_call_target="tpu_custom_call" | custom-call | tf_op jit(solution)/shard_map/gather_codes/pallas_call | solution.py:446
  52.5 6.7 %pass_column.2 = (f32[128,128]{1,0:T(8,128)S(1)}, f32[33280,128]{1,0:T(8,128)S(1)}) custom-call(s32[8,384]{1,0:T(8,128)S(1)} %get-tuple-element.14.lists_ref, bf16[4096,256]{1,0:T(8,128)(2,1)S(1)} %bitcast.18, bf16[32768,128]{1,0:T(8,128)(2,1)S(1)} %bitcast.17, f32[32,128]{1,0:T(8,128)S(1)} %bitcast.27, f32[128,128]{1,0:T(8,128)S(1)} %bitcast.22), custom_call_target="tpu_custom_call" | custom-call | flops 1073741824 | bytes 8388608 | tf_op jit(solution)/shard_map/pass_column/pallas_call | solution.py:148
  59.2 12.6 %column_exchange_0.1 = f32[16,8,128]{2,1,0:T(8,128)S(1)} custom-call(f32[16,8,128]{2,1,0:T(8,128)S(1)} %bitcast.26), custom_call_target="tpu_custom_call" | custom-call | tf_op jit(solution)/shard_map/column_exchange_0/pallas_call | solution.py:560
  71.8 2.8 %pass_row.1 = f32[1,32,128]{2,1,0:T(8,128)S(1)} custom-call(s32[8,384]{1,0:T(8,128)S(1)} %get-tuple-element.14.lists_ref, f32[33280,128]{1,0:T(8,128)S(1)} %get-tuple-element.19.refs_0_, f32[128,128]{1,0:T(8,128)S(1)} %bitcast.20), custom_call_target="tpu_custom_call" | custom-call | bytes 8388608 | tf_op jit(solution)/shard_map/pass_row/pallas_call | solution.py:148
  74.7 4.2 %row_exchange_0.1 = f32[2,16,128]{2,1,0:T(8,128)S(1)} custom-call(f32[1,2,16,128]{3,2,1,0:T(8,128)S(1)} %bitcast.24), custom_call_target="tpu_custom_call" | custom-call | tf_op jit(solution)/shard_map/row_exchange_0/pallas_call | solution.py:609
  78.8 2.9 %pass_column.3 = f32[128,128]{1,0:T(8,128)S(1)} custom-call(s32[8,384]{1,0:T(8,128)S(1)} %get-tuple-element.14.lists_ref, f32[33280,128]{1,0:T(8,128)S(1)} %get-tuple-element.19.refs_0_, f32[32,128]{1,0:T(8,128)S(1)} %bitcast.25), custom_call_target="tpu_custom_call" | custom-call | bytes 8388608 | tf_op jit(solution)/shard_map/pass_column/pallas_call | solution.py:148
  81.8 11.3 %column_exchange_1.1 = (f32[16,8,128]{2,1,0:T(8,128)S(1)}, f32[2,8,128]{2,1,0:T(8,128)S(1)}) custom-call(f32[16,8,128]{2,1,0:T(8,128)S(1)} %bitcast.19), custom_call_target="tpu_custom_call" | custom-call | tf_op jit(solution)/shard_map/column_exchange_1/pallas_call | solution.py:560
  93.1 3.9 %pass_final.1 = f32[2,32,128]{2,1,0:T(8,128)S(1)} custom-call(s32[8,384]{1,0:T(8,128)S(1)} %get-tuple-element.14.lists_ref, f32[33280,128]{1,0:T(8,128)S(1)} %get-tuple-element.19.refs_0_, f32[128,128]{1,0:T(8,128)S(1)} %bitcast.23), custom_call_target="tpu_custom_call" | custom-call | bytes 8388608 | tf_op jit(solution)/shard_map/pass_final/pallas_call | solution.py:148
  97.1 4.0 %row_exchange_1.1 = (f32[16,128]{1,0:T(8,128)S(1)}, f32[16,128]{1,0:T(8,128)S(1)}) custom-call(f32[2,2,16,128]{3,2,1,0:T(8,128)S(1)} %bitcast.21), custom_call_target="tpu_custom_call" | custom-call | tf_op jit(solution)/shard_map/row_exchange_1/pallas_call | solution.py:609
  101.0 0.6 copy.12
  101.6 0.6 copy.13
  102.2 0.6 copy.14

commit v6 on v5

--- a/solution.py
+++ b/solution.py
@@ -25,16 +25,13 @@
 
 def pass_kernel(kind, fresh, stored, lists_ref, *refs):
     refs = list(refs)
-    reads = stored and not fresh
-    if reads:
+    if stored:
         kept = refs.pop(0)
     else:
         u_ref, v_ref, unorm_ref, vnorm_ref = refs[:4]
         refs = refs[4:]
     pot_ref = None if fresh else refs.pop(0)
     out_ref = refs.pop(0)
-    if stored and fresh:
-        kept = refs.pop(0)
     sums_ref = refs.pop()
     if kind == "final":
         wsums_ref = refs.pop()
@@ -44,7 +41,7 @@
     by_column = kind == "column"
     roll_blocks = (refs[0] if refs else sums_ref).shape[0] // blk
 
-    if not reads:
+    if not stored:
         row_norm = refs.pop(0)
         feats = u_ref.shape[1]
         unit = SCALE / feats
@@ -59,7 +56,7 @@
 
         lax.fori_loop(0, roll_blocks, one, 0, unroll=8)
 
-    if not reads:
+    if not stored:
         spread(unorm_ref, -unit, row_norm)
     if by_column and not fresh:
         row_pot = refs.pop(0)
@@ -75,9 +72,8 @@
             t = lists_ref[1, at]
             live = jnp.where(at < total, SHIFT, -1e30)
             rows = pl.ds(pl.multiple_of(b * blk, blk), blk)
-            here = pl.ds(pl.multiple_of(at * blk, blk), blk)
-            if reads:
-                y = kept[here, :]
+            if stored:
+                y = kept[pl.ds(pl.multiple_of(lists_ref[3, at] * blk, blk), blk), :]
             else:
                 crossed = lax.dot_general(
                     u_ref[rows, :],
@@ -86,8 +82,6 @@
                     preferred_element_type=jnp.float32,
                 )
                 y = crossed * (2.0 * unit) + row_norm[rows, :] + vnorm_ref[pl.ds(t, 1), :] * (-unit)
-                if stored:
-                    kept[here, :] = y
             if by_column:
                 x = y + live if fresh else y + row_pot[rows, :] + live
                 parts.append((t, jnp.sum(jnp.exp2(x).reshape(blk // 8, 8, blk), axis=0)))
@@ -122,17 +116,15 @@
         lax.fori_loop(0, roll_blocks, finish, 0, unroll=8)
 
 
-def run_pass(kind, lists, u, v, unorm, vnorm, pot, kept, stored):
+def run_pass(kind, sizes, lists, data, pot, stored):
     fresh = pot is None
-    roll_blocks, blk = unorm.shape
-    targets = vnorm.shape[0]
+    roll_blocks, targets, blk = sizes
     pairs = lists.shape[1] - 128
     smem = pl.BlockSpec(memory_space=pltpu.SMEM)
     vmem = pl.BlockSpec(memory_space=pltpu.VMEM)
     frames = pltpu.VMEM((roll_blocks * blk, blk), jnp.float32)
     by_column = kind == "column"
-    reads = stored and not fresh
-    args = [kept] if reads else [u, v, unorm, vnorm]
+    args = list(data)
     if not fresh:
         args.append(pot)
     if by_column:
@@ -141,9 +133,7 @@
     else:
         outs = [jax.ShapeDtypeStruct((2 if kind == "final" else 1, roll_blocks, blk), jnp.float32)]
         sums = [frames] * (2 if kind == "final" else 1)
-    if stored and fresh:
-        outs.append(jax.ShapeDtypeStruct(((pairs + UNROLL) * blk, blk), jnp.float32))
-    scratch = ([] if reads else [frames]) + ([frames] if by_column and not fresh else []) + sums
+    scratch = ([] if stored else [frames]) + ([frames] if by_column and not fresh else []) + sums
     held = sum(math.prod(a.shape) * a.dtype.itemsize for a in scratch + ([] if stored else args + outs))
     return pl.pallas_call(
         functools.partial(pass_kernel, kind, fresh, stored),
@@ -153,8 +143,8 @@
         scratch_shapes=scratch,
         compiler_params=pltpu.CompilerParams(vmem_limit_bytes=held + 2 * MIB),
         cost_estimate=pl.CostEstimate(
-            flops=0 if reads else pairs * blk * blk * u.shape[1],
-            bytes_accessed=2 * v.size,
+            flops=pairs * blk * blk * (4 if stored else data[0].shape[1]),
+            bytes_accessed=pairs * blk * blk * 4,
             transcendentals=pairs * blk * blk // 2,
         ),
         name="pass_" + kind,
@@ -215,51 +205,70 @@
     return total[0:1, :]
 
 
-def packed_pairs(pairs, location, slots, demo_count, share, part, width):
+def packed_pairs(pairs, location, slots, demo_count, share, part, reps, capacity, width):
     blocks = pairs.shape[0]
-    names = lax.broadcasted_iota(jnp.int32, (blocks, 128), 1).astype(jnp.float32)
-    places = lax.broadcasted_iota(jnp.int32, (blocks, width), 1).astype(jnp.float32)
-    number = lax.broadcasted_iota(jnp.int32, (blocks, width), 0).astype(jnp.float32)
+    own_blocks = blocks // reps
+    names = lax.broadcasted_iota(jnp.int32, (blocks, 128), 1)
+    places = lax.broadcasted_iota(jnp.int32, (blocks, width), 1)
+    block = lax.broadcasted_iota(jnp.int32, (blocks, 1), 0)
+    side_of = lax.div(block, jnp.int32(own_blocks))
     count = pairs[:, slots : slots + 1]
-    where_held = location.astype(jnp.float32)
-    mine, target = [], []
+    mine, owners, locals_, chosen = [], [], [], []
     for s in range(slots):
-        found = jnp.zeros((blocks, 128), jnp.float32)
+        found = jnp.zeros((blocks, 128), jnp.int32)
         for k in range(location.shape[0]):
-            hit = pairs[:, s : s + 1] - 128.0 * k == names
-            found = found + jnp.where(hit, where_held[k : k + 1, :], 0.0)
+            hit = pairs[:, s : s + 1] - 128 * k == names
+            found = found + jnp.where(hit, location[k : k + 1, :], 0)
         stored = jnp.sum(found, axis=1, keepdims=True)
-        owner = jnp.floor((stored + 0.5) * (1.0 / demo_count))
+        owner = lax.div(stored, jnp.int32(demo_count))
         local = stored - owner * demo_count
-        side = jnp.floor((local + 0.5) * (1.0 / share))
-        mine.append(jnp.where((count > s) & (side == part.astype(jnp.float32)), 1.0, 0.0))
-        target.append(owner * share + local - side * share)
+        side = lax.div(local, jnp.int32(share))
+        use = (count > s) & (side == part)
+        mine.append(jnp.where(use, 1, 0))
+        owners.append(owner)
+        locals_.append(local - side * share)
+        chosen.append(jnp.where((owner == names) & use, 1, 0))
     in_row = sum(mine)
-    below = lax.broadcasted_iota(jnp.int32, (blocks, blocks), 1) < lax.broadcasted_iota(jnp.int32, (blocks, blocks), 0)
-    spread = jnp.broadcast_to(in_row, (blocks, 128)).astype(jnp.bfloat16)
-    before = jnp.dot(below.astype(jnp.float32).astype(jnp.bfloat16), spread, preferred_element_type=jnp.float32)
+    of_owner = sum(chosen)
+    rows_wide = lax.broadcasted_iota(jnp.int32, (blocks, 128), 0)
+    in_wide = jnp.broadcast_to(in_row, (blocks, 128))
+    before = jnp.zeros((blocks, 128), jnp.int32)
+    running = jnp.zeros((blocks, 128), jnp.int32)
+    for b in range(blocks - 1):
+        after = rows_wide > b
+        near = after & (rows_wide < (b // own_blocks + 1) * own_blocks)
+        before = before + jnp.where(after, in_wide[b : b + 1, :], 0)
+        running = running + jnp.where(near, of_owner[b : b + 1, :], 0)
     rank = before[:, 0:1]
-    homes = jnp.zeros((blocks, width), jnp.float32)
-    targets = jnp.zeros((blocks, width), jnp.float32)
+    rows = [jnp.zeros((blocks, width), jnp.int32) for _ in range(5)]
     for s in range(slots):
-        hit = (rank == places) & (mine[s] > 0.5)
-        homes = homes + jnp.where(hit, number, 0.0)
-        targets = targets + jnp.where(hit, target[s], 0.0)
+        own_rank = jnp.sum(running * chosen[s], axis=1, keepdims=True)
+        place = (owners[s] * reps + side_of) * capacity + own_rank
+        hit = (rank == places) & (mine[s] > 0)
+        at_place = (place == places) & (mine[s] > 0)
+        values = (block, owners[s] * share + locals_[s], place, block - side_of * own_blocks, locals_[s])
+        for k, value in enumerate(values):
+            rows[k] = rows[k] + jnp.where(hit if k < 3 else at_place, value, 0)
         rank = rank + mine[s]
-    total = jnp.sum(jnp.broadcast_to(in_row, (blocks, width)), axis=0, keepdims=True)
-    rows = [jnp.sum(homes, axis=0, keepdims=True), jnp.sum(targets, axis=0, keepdims=True), total]
-    return [row.astype(jnp.int32) for row in rows]
+        running = running + chosen[s]
+    total = jnp.broadcast_to(in_row, (blocks, width))
+    rows = [rows[0], rows[1], total, rows[2], rows[3], rows[4]]
+    return [jnp.sum(r, axis=0, keepdims=True) for r in rows]
 
 
 def gather_kernel(n, reps, slots, *refs):
-    demo, rollout, projection_hbm, pair_block, pair_count, location_hbm = refs[:6]
-    v, vnorm, u, unorm, lists = refs[6:11]
-    (demo_in, rollout_in, projection, location, block_in, count_in, own_pairs, own_v, own_vnorm, own_u, own_unorm, pairs,
-     ring_send, ring_recv, side_send, side_recv, norm_send, norm_recv, rep_send, rep_recv, home) = refs[11:]
+    demo, rollout, projection_hbm, pair_block, pair_count, location_hbm, costs, lists = refs[:8]
+    hops = n // 4
+    refs = list(refs[8:])
+    own_slots, twin_slots = refs[: 2 * hops - 1], refs[2 * hops - 1 : 4 * hops - 1]
+    refs = refs[4 * hops - 1 :]
+    u_slots, norm_slots = refs[: reps - 1], refs[reps - 1 : 2 * (reps - 1)]
+    row_terms = refs[2 * (reps - 1) : 3 * reps - 2]
+    (demo_in, rollout_in, projection, location, block_in, count_in, own_pairs, own_v, own_vnorm, vnorm, own_u, own_unorm,
+     pairs, known, ring_send, ring_recv, side_send, side_recv, norm_send, norm_recv, rep_send, rep_recv, home) = refs[3 * reps - 2 :]
     me = lax.axis_index("roll")
     part = lax.axis_index("rep")
     chips = n // 2
-    hops = chips // 2
     core = lax.rem(me, 2)
     chip = me // 2
     odd = lax.rem(chip, 2)
@@ -276,11 +285,13 @@
     feats = projection.shape[1]
     share, blk = own_vnorm.shape
     own_blocks = own_unorm.shape[0]
+    capacity = max(1, own_blocks * slots // n)
+    unit = SCALE / feats
     near = others("roll", n) + others("rep", reps)
-    fetch_demo = pltpu.make_async_copy(demo.at[pl.ds(part * (share * blk), share * blk)], demo_in, home.at[4])
+    fetch_demo = pltpu.make_async_copy(demo.at[pl.ds(part * (share * blk), share * blk)], demo_in, home.at[0])
     fetch_demo.start()
     fetches = [
-        pltpu.make_async_copy(source, target, home.at[6 + k])
+        pltpu.make_async_copy(source, target, home.at[2 + k])
         for k, (source, target) in enumerate((
             (projection_hbm, projection),
             (pair_block, block_in),
@@ -290,82 +301,78 @@
     ]
     for fetch in fetches:
         fetch.start()
-    fetch_rollout = pltpu.make_async_copy(rollout, rollout_in, home.at[5])
+    fetch_rollout = pltpu.make_async_copy(rollout, rollout_in, home.at[1])
     fetch_rollout.start()
     barrier = pltpu.get_barrier_semaphore()
     for partner in near:
         pl.semaphore_signal(barrier, inc=1, device_id=partner, device_id_type=MESH)
-    fetch_demo.wait()
     for fetch in fetches:
         fetch.wait()
     own_pairs[...] = jnp.zeros_like(own_pairs)
     own_pairs[0:slots, 0 : block_in.shape[1]] = block_in[...]
     own_pairs[slots : slots + 1, 0 : count_in.shape[1]] = count_in[...]
     turned = jnp.transpose(projection[...])
+    fetch_demo.wait()
     for b in range(share):
-        own_v[b * feats : (b + 1) * feats, :] = lax.dot_general(
+        own_v[b] = lax.dot_general(
             turned, demo_in[b * blk : (b + 1) * blk, :], (((1,), (1,)), ((), ())),
             preferred_element_type=jnp.float32,
         ).astype(jnp.bfloat16)
     pl.semaphore_wait(barrier, len(near))
 
-    waits = []
-
-    def origin(way, s):
-        return at_place(place - s) if way == 0 else at_place(place + s)
-
-    def chunk(s, way, half):
-        piece = pl.ds(half * rows, rows)
+    def own_slot(way, s):
         if s == 0:
-            return own_v.at[piece], v.at[me, piece]
-        block = origin(way, s)
-        return v.at[block, piece], v.at[block, piece]
-
-    def send(s, way, half):
-        source, target = chunk(s, way, half)
+            return own_v
+        return own_slots[2 * (hops - 1) if s == hops else way * (hops - 1) + s - 1]
+
+    def twin_slot(way, s):
+        if s == 0:
+            return twin_slots[2 * hops - 1]
+        return twin_slots[2 * (hops - 1) if s == hops else way * (hops - 1) + s - 1]
+
+    def remote(source, target, sends, recvs, device):
         copy = pltpu.make_async_remote_copy(
-            src_ref=source, dst_ref=target,
-            send_sem=ring_send.at[way, s, half], recv_sem=ring_recv.at[way, s, half],
-            device_id=ways[way], device_id_type=MESH,
+            src_ref=source, dst_ref=target, send_sem=sends, recv_sem=recvs, device_id=device, device_id_type=MESH
         )
         copy.start()
         return copy
 
-    def cross(s, way, half):
-        source, target = chunk(s, way, half)
-        copy = pltpu.make_async_remote_copy(
-            src_ref=source, dst_ref=target,
-            send_sem=side_send.at[way, s, half], recv_sem=side_recv.at[way, s, half],
-            device_id=twin, device_id_type=MESH,
+    def send(s, way, q):
+        piece = pl.ds(q * rows, rows)
+        return remote(
+            own_slot(way, s).at[piece], own_slot(way, s + 1).at[piece],
+            ring_send.at[way, s, q], ring_recv.at[way, s, q], ways[way],
         )
-        copy.start()
-        waits.append(copy)
-
-    def travels(s, way, half):
-        return s < hops - 1 or (s == hops - 1 and half * 2 // CHUNKS == way)
+
+    crossing = {}
+
+    def cross(s, way, q):
+        piece = pl.ds(q * rows, rows)
+        copy = remote(
+            own_slot(way, s).at[piece], twin_slot(way, s).at[piece],
+            side_send.at[way, s, q], side_recv.at[way, s, q], twin,
+        )
+        crossing.setdefault((0 if s == hops else way, s), []).append(copy)
+
+    def travels(s, way, q):
+        return s < hops - 1 or (s == hops - 1 and q * 2 // CHUNKS == way)
 
     moving = {}
-    for half in range(CHUNKS):
+    for q in range(CHUNKS):
         for way in range(2):
-            if travels(0, way, half):
-                moving[0, way, half] = send(0, way, half)
-
-    def spread(source, target, axis, which, sends, recvs):
-        started = []
-        for d, partner in enumerate(others(axis, reps if axis == "rep" else n)):
-            copy = pltpu.make_async_remote_copy(
-                src_ref=source, dst_ref=target,
-                send_sem=sends.at[which, d], recv_sem=recvs.at[which, d],
-                device_id=partner, device_id_type=MESH,
-            )
-            copy.start()
-            started.append(copy)
-        return started
-
-    pair_copies = spread(own_pairs, pairs.at[part], "rep", 0, rep_send, rep_recv)
+            if travels(0, way, q):
+                moving[0, way, q] = send(0, way, q)
+
+    def to_reps(source, targets, which):
+        return [
+            remote(source, targets[d], rep_send.at[which, d], rep_recv.at[which, d], partner)
+            for d, partner in enumerate(others("rep", reps))
+        ]
+
+    pair_copies = to_reps(own_pairs, [pairs.at[part]] * (reps - 1), 0)
     pairs[part] = own_pairs[...]
-    for half in range(CHUNKS):
-        cross(0, 0, half)
+    for q in range(CHUNKS):
+        cross(0, 0, q)
     fetch_rollout.wait()
 
     def do_rollout(b, carry):
@@ -373,61 +380,123 @@
         codes = jnp.dot(
             rollout_in[rows_b, :], projection[...], preferred_element_type=jnp.float32
         ).astype(jnp.bfloat16)
-        own_u[rows_b, :] = codes
+        own_u[b] = codes
         own_unorm[pl.ds(b, 1), :] = block_norms(codes)
         return carry
 
     lax.fori_loop(0, own_blocks, do_rollout, 0)
-
-    def send_rollout(q):
-        piece = pl.ds(q * (own_u.shape[0] // hops), own_u.shape[0] // hops)
-        return spread(own_u.at[piece], u.at[part, piece], "rep", 2 + q, rep_send, rep_recv)
-
-    waits += send_rollout(0)
-    waits += spread(own_unorm, unorm.at[part], "rep", 1, rep_send, rep_recv)
+    frame_copies = to_reps(own_u, u_slots, 2) + to_reps(own_unorm, norm_slots, 1)
 
     def do_demo(b, carry):
-        wide = own_v[pl.ds(pl.multiple_of(b * feats, feats), feats), :].astype(jnp.float32)
+        wide = own_v[b].astype(jnp.float32)
         own_vnorm[pl.ds(b, 1), :] = jnp.sum(wide * wide, axis=0, keepdims=True)
         return carry
 
     lax.fori_loop(0, share, do_demo, 0)
-    waits += spread(own_vnorm, vnorm.at[me], "roll", 0, norm_send, norm_recv)
-    stays = []
-    for k, (source, target) in enumerate(
-        ((own_v, v.at[me]), (own_vnorm, vnorm.at[me]), (own_u, u.at[part]), (own_unorm, unorm.at[part]))
-    ):
-        copy = pltpu.make_async_copy(source, target, home.at[k])
-        copy.start()
-        stays.append(copy)
+    vnorm_copies = [
+        remote(own_vnorm, vnorm.at[me], norm_send.at[d], norm_recv.at[d], partner)
+        for d, partner in enumerate(others("roll", n))
+    ]
+    vnorm[me] = own_vnorm[...]
+
+    def spread_norms(source, target):
+        def one(b, carry):
+            line = source[pl.ds(b, 1), :] * (-unit)
+            target[b] = jnp.transpose(jnp.broadcast_to(line, (blk, blk)))
+            return carry
+
+        lax.fori_loop(0, own_blocks, one, 0, unroll=4)
+
+    spread_norms(own_unorm, row_terms[0])
     for copy in pair_copies:
         copy.wait()
     square = [
-        jnp.concatenate([pairs[r].astype(jnp.float32), jnp.zeros((128 - pairs.shape[1], 128), jnp.float32)], axis=0)
+        jnp.concatenate([pairs[r], jnp.zeros((128 - pairs.shape[1], 128), jnp.int32)], axis=0)
         for r in range(reps)
     ]
     everyone = jnp.concatenate([jnp.transpose(a)[0:own_blocks, :] for a in square], axis=0)
-    found = packed_pairs(everyone, location[...], slots, share * reps, share, part, lists.shape[1])
+    found = packed_pairs(
+        everyone, location[...], slots, share * reps, share, part, reps, capacity, lists.shape[1]
+    )
     lists[...] = jnp.zeros_like(lists)
     for k, row in enumerate(found):
         lists[k : k + 1, :] = row
+    to_scalars = pltpu.make_async_copy(lists, known, home.at[6])
+    to_scalars.start()
+    to_scalars.wait()
+    for copy in vnorm_copies:
+        copy.wait_recv()
+
+    met = set()
+
+    def work(way, s, far_side, other):
+        slot = (twin_slot if far_side else own_slot)(way, s)
+        owner = at_place(place - s) if way == 0 else at_place(place + s)
+        if far_side:
+            owner = owner + 1 - 2 * core
+            if (way, s) not in met:
+                met.add((way, s))
+                for copy in crossing[way, s]:
+                    copy.wait_recv()
+        if other and other not in met:
+            met.add(other)
+            for copy in frame_copies[other - 1 :: reps - 1]:
+                copy.wait_recv()
+            spread_norms(norm_slots[other - 1], row_terms[other])
+        codes = u_slots[other - 1] if other else own_u
+        rep = lax.rem(part - other + reps, reps)
+        first = (owner * reps + rep) * capacity
+
+        def tile(k, carry):
+            at = first + k
+            b = known[4, at]
+            t = known[5, at]
+            crossed = jnp.dot(codes[b], slot[t], preferred_element_type=jnp.float32)
+            costs[pl.ds(pl.multiple_of(at * blk, blk), blk), :] = (
+                crossed * (2.0 * unit) + row_terms[other][b] + vnorm[owner, t].reshape(1, blk) * (-unit)
+            )
+            return carry
+
+        lax.fori_loop(0, capacity, tile, 0, unroll=min(4, capacity))
+
+    queue, later = [], []
+
+    def ready(s):
+        for far_side in (False, True):
+            for way in range(1 if s in (0, hops) else 2):
+                queue.append((way, s, far_side, 0))
+                for other in range(1, reps):
+                    (later if s < 2 else queue).append((way, s, far_side, other))
+
+    def run(most):
+        for _ in range(min(most, len(queue))):
+            work(*queue.pop(0))
+
+    ready(0)
+    run(1)
     for s in range(1, hops + 1):
-        for half in range(CHUNKS):
+        if s == hops - 1:
+            queue[:0] = later
+        half = CHUNKS // 2
+        order = range(CHUNKS) if s < hops else [q // 2 + half * (q % 2) for q in range(CHUNKS)]
+        for q in order:
             for way in range(2):
-                if (s - 1, way, half) not in moving:
+                if (s - 1, way, q) not in moving:
                     continue
-                moving[s - 1, way, half].wait_recv()
-                if travels(s, way, half):
-                    moving[s, way, half] = send(s, way, half)
-                cross(s, way, half)
-        if s < hops:
-            waits += send_rollout(s)
+                moving[s - 1, way, q].wait_recv()
+                if travels(s, way, q):
+                    moving[s, way, q] = send(s, way, q)
+                cross(s, way, q)
+            run(4 if s < hops else 2)
+        ready(s)
+    run(len(queue))
     for copy in moving.values():
         copy.wait_send()
-    for copy in stays:
-        copy.wait()
-    for copy in waits:
-        copy.wait()
+    for copies in crossing.values():
+        for copy in copies:
+            copy.wait_send()
+    for copy in frame_copies + vnorm_copies:
+        copy.wait_send()
 
 
 def gathered(n, reps, demo, rollout, projection, pair_block, pair_count, location):
@@ -436,47 +505,52 @@
     blk = rollout.shape[0] // own_blocks
     feats = projection.shape[1]
     share = demo.shape[0] // blk // reps
+    places = n * reps * max(1, own_blocks * slots // n)
     location = location.reshape(-1, 128)
     own_pairs = (slots // 8 * 8 + 8, 128)
     hbm = pl.BlockSpec(memory_space=pltpu.HBM)
-    anywhere = pl.BlockSpec(memory_space=pl.ANY)
     vmem = pl.BlockSpec(memory_space=pltpu.VMEM)
     dma = pltpu.SemaphoreType.DMA
     wide, code = jnp.float32, jnp.bfloat16
+    slot = pltpu.VMEM((share, feats, blk), code)
+    frames = pltpu.VMEM((own_blocks, blk, feats), code)
+    scratch = [slot] * (4 * hops - 1) + [frames] * (reps - 1) + [pltpu.VMEM((own_blocks, blk), wide)] * (reps - 1)
+    scratch += [pltpu.VMEM((own_blocks, blk, blk), wide)] * reps
+    scratch += [
+        pltpu.VMEM((share * blk, feats), code),
+        pltpu.VMEM(rollout.shape, code),
+        pltpu.VMEM(projection.shape, code),
+        pltpu.VMEM(location.shape, jnp.int32),
+        pltpu.VMEM((slots, own_blocks), jnp.int32),
+        pltpu.VMEM((1, own_blocks), jnp.int32),
+        pltpu.VMEM(own_pairs, jnp.int32),
+        slot,
+        pltpu.VMEM((share, blk), wide),
+        pltpu.VMEM((n, share, blk), wide),
+        frames,
+        pltpu.VMEM((own_blocks, blk), wide),
+        pltpu.VMEM((reps,) + own_pairs, jnp.int32),
+    ]
+    held = sum(math.prod(a.shape) * a.dtype.itemsize for a in scratch)
+    lists = jax.ShapeDtypeStruct((8, places + 128), jnp.int32)
+    scratch += [
+        pltpu.SMEM(lists.shape, jnp.int32),
+        dma((2, hops, CHUNKS)), dma((2, hops, CHUNKS)),
+        dma((2, hops + 1, CHUNKS)), dma((2, hops + 1, CHUNKS)),
+        dma((n - 1,)), dma((n - 1,)),
+        dma((3, reps - 1)), dma((3, reps - 1)),
+        dma((7,)),
+    ]
     return pl.pallas_call(
         functools.partial(gather_kernel, n, reps, slots),
-        out_shape=[
-            jax.ShapeDtypeStruct((n, share * feats, blk), code),
-            jax.ShapeDtypeStruct((n, share, blk), wide),
-            jax.ShapeDtypeStruct((reps, own_blocks * blk, feats), code),
-            jax.ShapeDtypeStruct((reps, own_blocks, blk), wide),
-            jax.ShapeDtypeStruct((8, reps * own_blocks * slots + 128), jnp.int32),
-        ],
+        out_shape=[jax.ShapeDtypeStruct((places * blk, blk), wide), lists],
         in_specs=[hbm] * 6,
-        out_specs=[anywhere] * 4 + [vmem],
-        scratch_shapes=[
-            pltpu.VMEM((share * blk, feats), code),
-            pltpu.VMEM(rollout.shape, code),
-            pltpu.VMEM(projection.shape, code),
-            pltpu.VMEM(location.shape, jnp.int32),
-            pltpu.VMEM((slots, own_blocks), jnp.int32),
-            pltpu.VMEM((1, own_blocks), jnp.int32),
-            pltpu.VMEM(own_pairs, jnp.int32),
-            pltpu.VMEM((share * feats, blk), code),
-            pltpu.VMEM((share, blk), wide),
-            pltpu.VMEM((own_blocks * blk, feats), code),
-            pltpu.VMEM((own_blocks, blk), wide),
-            pltpu.VMEM((reps,) + own_pairs, jnp.int32),
-            dma((2, hops, CHUNKS)), dma((2, hops, CHUNKS)),
-            dma((2, hops + 1, CHUNKS)), dma((2, hops + 1, CHUNKS)),
-            dma((1, n - 1)), dma((1, n - 1)),
-            dma((2 + hops, reps - 1)), dma((2 + hops, reps - 1)),
-            dma((10,)),
-        ],
+        out_specs=[vmem] * 2,
+        scratch_shapes=scratch,
         compiler_params=pltpu.CompilerParams(
-            collective_id=0, has_side_effects=True, vmem_limit_bytes=8 * MIB
+            collective_id=0, has_side_effects=True, vmem_limit_bytes=held + 3 * MIB
         ),
-        name="gather_codes",
+        name="gather_costs",
     )(*(
         pltpu.with_memory_space_constraint(a, pltpu.HBM)
         for a in (demo, rollout, projection, pair_block.T, pair_count[None, :], location)
@@ -620,17 +694,19 @@
 
 
 def body(rollout, demo, projection, location, pair_block, pair_count):
-    blk = rollout.shape[0] // pair_block.shape[0]
+    own_blocks = pair_block.shape[0]
+    blk = rollout.shape[0] // own_blocks
     n = lax.axis_size("roll")
     reps = lax.axis_size("rep")
-    if n <= DIRECT:
-        v, vnorm, u, unorm, lists = gathered(
-            n, reps, demo, rollout, projection, pair_block, pair_count, location
-        )
+    demo_count = demo.shape[0] // blk
+    share = demo_count // reps
+    sizes = (reps * own_blocks, n * share, blk)
+    stored = n <= DIRECT
+    if stored:
+        costs, lists = gathered(n, reps, demo, rollout, projection, pair_block, pair_count, location)
+        data = (costs,)
     else:
         part = lax.axis_index("rep")
-        demo_count = demo.shape[0] // blk
-        share = demo_count // reps
         own_demo = lax.dynamic_slice_in_dim(demo, part * (share * blk), share * blk, 0)
         own_v = project(own_demo, projection)
         own_u = project(rollout, projection)
@@ -639,18 +715,16 @@
         u, unorm = (lax.all_gather(a, "rep") for a in (own_u, norms(own_u, blk)))
         pairs, counts = (lax.all_gather(a, "rep", tiled=True) for a in (pair_block, pair_count))
         lists = listed(pairs, counts, location, demo_count, share, part)
-    v, vnorm, u, unorm = (a.reshape(-1, a.shape[-1]) for a in (v, vnorm, u, unorm))
-
-    stored = n <= DIRECT
-    roll_pot = kept = None
+        data = tuple(a.reshape(-1, a.shape[-1]) for a in (u, v, unorm, vnorm))
+
+    roll_pot = None
     for iteration in range(ITERS):
-        sums, *rest = run_pass("column", lists, u, v, unorm, vnorm, roll_pot, kept, stored)
-        kept = rest[0] if rest else kept
+        sums = run_pass("column", sizes, lists, data, roll_pot, stored)[0]
         demo_pot, held_pot = column_potentials(n, reps, sums, iteration)
         kind = "final" if iteration == ITERS - 1 else "row"
-        sums = run_pass(kind, lists, u, v, unorm, vnorm, demo_pot, kept, stored)[0]
+        sums = run_pass(kind, sizes, lists, data, demo_pot, stored)[0]
         results = row_totals(reps, sums, iteration)
-        roll_pot = results[0].reshape(unorm.shape) if kind == "row" else None
+        roll_pot = results[0].reshape(-1, blk) if kind == "row" else None
     return results[0].reshape(-1), results[1].reshape(-1), held_pot.reshape(-1)
 
 

time: 103 us -> 102 us (level)
  Pallas kernels: 100 us -> 98.7 us
    pallas_call x1, Pallas kernels: 51.8 us -> 56.6 us  [gathered(): pl.pallas_call(functools.partial(gather_kernel, n, reps, slots), out_shap...]
    pallas_call x4, Pallas kernels: 16.4 us -> 12.3 us  [run_pass(): pl.pallas_call(functools.partial(pass_kernel, kind, fresh, stored), out_s...]
    pallas_call x2, Pallas kernels: 24 us -> 22 us  [column_potentials(): pl.pallas_call(functools.partial(column_kernel, n, reps if last else 0),...]
where the time goes in v6:
time: 102 us; the launch traced here: 101 us
  Pallas kernels  98.7 us (97%)
  local copies, waits for them, and re-layouts  1.8 us (2%)
    pallas_call x1, Pallas kernels, gathered(): pl.pallas_call(functools.partial(gather_kernel, n, reps, slots), out_shap...  56.6 us
    pallas_call x2, Pallas kernels, column_potentials(): pl.pallas_call(functools.partial(column_kernel, n, reps if last else 0),...  22 us
    pallas_call x4, Pallas kernels, run_pass(): pl.pallas_call(functools.partial(pass_kernel, kind, fresh, stored), out_s...  12.3 us
    pallas_call x2, Pallas kernels, row_totals(): pl.pallas_call(functools.partial(row_kernel, reps, last), out_shape=[jax....  7.78 us

profile of v6, /device:TPU:0, one launch (start us, length us, event | category | flops | bytes accessed | tf_op | source)
XLA Modules:
  0.0 101.2 jit_solution(16717615316498157489)
XLA Ops:
  0.6 56.6 %gather_costs.1 = (f32[32768,128]{1,0:T(8,128)S(1)}, s32[8,384]{1,0:T(8,128)S(1)}) custom-call(bf16[2048,256]{1,0:T(8,128)(2,1)} %refs_0_.1, bf16[2048,256]{1,0:T(8,128)(2,1)} %refs_1_.1, bf16[256,256]{1,0:T(8,128)(2,1)} %refs_2_.1, s32[8,16]{1,0:T(8,128)} %bitcast.23, s32[1,16]{1,0:T(1,128)} %bitcast.25, s32[2,128]{1,0:T(2,128)} %bitcast.24), custom_call_target="tpu_custom_call" | custom-call | tf_op jit(solution)/shard_map/gather_costs/pallas_call | solution.py:544
  57.2 2.2 %pass_column.2 = f32[128,128]{1,0:T(8,128)S(1)} custom-call(s32[8,384]{1,0:T(8,128)S(1)} %get-tuple-element.9.lists_ref, f32[32768,128]{1,0:T(8,128)S(1)} %get-tuple-element.10.refs_0_), custom_call_target="tpu_custom_call" | custom-call | flops 16777216 | bytes 16777216 | tf_op jit(solution)/shard_map/pass_column/pallas_call | solution.py:138
  59.4 11.9 %column_exchange_0.1 = f32[16,8,128]{2,1,0:T(8,128)S(1)} custom-call(f32[16,8,128]{2,1,0:T(8,128)S(1)} %bitcast.15), custom_call_target="tpu_custom_call" | custom-call | tf_op jit(solution)/shard_map/column_exchange_0/pallas_call | solution.py:634
  71.3 3.0 %pass_row.1 = f32[1,32,128]{2,1,0:T(8,128)S(1)} custom-call(s32[8,384]{1,0:T(8,128)S(1)} %get-tuple-element.9.lists_ref, f32[32768,128]{1,0:T(8,128)S(1)} %get-tuple-element.10.refs_0_, f32[128,128]{1,0:T(8,128)S(1)} %bitcast.14), custom_call_target="tpu_custom_call" | custom-call | flops 16777216 | bytes 16777216 | tf_op jit(solution)/shard_map/pass_row/pallas_call | solution.py:138
  74.3 3.8 %row_exchange_0.1 = f32[2,16,128]{2,1,0:T(8,128)S(1)} custom-call(f32[1,2,16,128]{3,2,1,0:T(8,128)S(1)} %bitcast.18), custom_call_target="tpu_custom_call" | custom-call | tf_op jit(solution)/shard_map/row_exchange_0/pallas_call | solution.py:683
  78.1 3.1 %pass_column.3 = f32[128,128]{1,0:T(8,128)S(1)} custom-call(s32[8,384]{1,0:T(8,128)S(1)} %get-tuple-element.9.lists_ref, f32[32768,128]{1,0:T(8,128)S(1)} %get-tuple-element.10.refs_0_, f32[32,128]{1,0:T(8,128)S(1)} %bitcast.19), custom_call_target="tpu_custom_call" | custom-call | flops 16777216 | bytes 16777216 | tf_op jit(solution)/shard_map/pass_column/pallas_call | solution.py:138
  81.2 10.2 %column_exchange_1.1 = (f32[16,8,128]{2,1,0:T(8,128)S(1)}, f32[2,8,128]{2,1,0:T(8,128)S(1)}) custom-call(f32[16,8,128]{2,1,0:T(8,128)S(1)} %bitcast.13), custom_call_target="tpu_custom_call" | custom-call | tf_op jit(solution)/shard_map/column_exchange_1/pallas_call | solution.py:634
  91.4 4.0 %pass_final.1 = f32[2,32,128]{2,1,0:T(8,128)S(1)} custom-call(s32[8,384]{1,0:T(8,128)S(1)} %get-tuple-element.9.lists_ref, f32[32768,128]{1,0:T(8,128)S(1)} %get-tuple-element.10.refs_0_, f32[128,128]{1,0:T(8,128)S(1)} %bitcast.17), custom_call_target="tpu_custom_call" | custom-call | flops 16777216 | bytes 16777216 | tf_op jit(solution)/shard_map/pass_final/pallas_call | solution.py:138
  95.4 4.0 %row_exchange_1.1 = (f32[16,128]{1,0:T(8,128)S(1)}, f32[16,128]{1,0:T(8,128)S(1)}) custom-call(f32[2,2,16,128]{3,2,1,0:T(8,128)S(1)} %bitcast.16), custom_call_target="tpu_custom_call" | custom-call | tf_op jit(solution)/shard_map/row_exchange_1/pallas_call | solution.py:683
  99.4 0.6 copy.12
  100.0 0.6 copy.13
  100.6 0.6 copy.14

commit v7 on v6

--- a/solution.py
+++ b/solution.py
@@ -457,7 +457,7 @@
             )
             return carry
 
-        lax.fori_loop(0, capacity, tile, 0, unroll=min(4, capacity))
+        lax.fori_loop(0, capacity, tile, 0, unroll=min(8 if s == hops else 4, capacity))
 
     queue, later = [], []
 
@@ -487,7 +487,7 @@
                 if travels(s, way, q):
                     moving[s, way, q] = send(s, way, q)
                 cross(s, way, q)
-            run(4 if s < hops else 2)
+            run(4 if s < hops else 3 if q % half == 0 else 0)
         ready(s)
     run(len(queue))
     for copy in moving.values():
@@ -559,54 +559,65 @@
 
 def column_kernel(n, reps, sums, *refs):
     if reps:
-        out, both, landed, full, held, first_send, first_recv, second_send, second_recv, rep_send, rep_recv = refs
+        out, both, from_twin, added, landed, full, held, *sems, rep_send, rep_recv = refs
     else:
-        out, landed, full, first_send, first_recv, second_send, second_recv = refs
+        out, from_twin, added, landed, full, *sems = refs
+    first_send, first_recv, second_send, second_recv, twin_send, twin_recv = sems
     me = lax.axis_index("roll")
-    partners = others("roll", n)
+    chips = n // 2
+    core = lax.rem(me, 2)
+    chip = me // 2
+    twin = {"roll": me + 1 - 2 * core}
+    peers = [lax.rem(chip + d, chips) for d in range(1, chips)]
+    partners = [{"roll": peer * 2 + core} for peer in peers]
     twins = others("rep", reps) if reps else []
-    greet(partners + twins)
-    copies = []
-    for d, partner in enumerate(partners):
+    greet([twin] + partners + twins)
+
+    def remote(source, target, sends, recvs, device):
         copy = pltpu.make_async_remote_copy(
-            src_ref=sums.at[partner["roll"]], dst_ref=landed.at[d],
-            send_sem=first_send.at[d], recv_sem=first_recv.at[d],
-            device_id=partner, device_id_type=MESH,
+            src_ref=source, dst_ref=target, send_sem=sends, recv_sem=recvs, device_id=device, device_id_type=MESH
         )
         copy.start()
-        copies.append(copy)
-    total = sums[me]
-    for d, copy in enumerate(copies):
+        return copy
+
+    across = [
+        remote(sums.at[c, 1 - core], from_twin.at[c], twin_send.at[c], twin_recv.at[c], twin) for c in range(chips)
+    ]
+    for copy in across:
+        copy.wait_recv()
+    added[...] = from_twin[...] + sums[:, core]
+    firsts = [
+        remote(added.at[peer], landed.at[d], first_send.at[d], first_recv.at[d], partners[d])
+        for d, peer in enumerate(peers)
+    ]
+    total = added[chip]
+    for d, copy in enumerate(firsts):
         copy.wait_recv()
         total = total + landed[d]
     pot = SHIFT - jnp.log2(total + FLOOR)
-    full[me] = pot
-    seconds = []
-    for d, partner in enumerate(partners):
-        copy = pltpu.make_async_remote_copy(
-            src_ref=full.at[me], dst_ref=full.at[me],
-            send_sem=second_send.at[d], recv_sem=second_recv.at[d],
-            device_id=partner, device_id_type=MESH,
-        )
-        copy.start()
-        seconds.append(copy)
+    full[core, chip] = pot
+    seconds = [
+        remote(full.at[core, chip], full.at[core, chip], second_send.at[d], second_recv.at[d], partner)
+        for d, partner in enumerate(partners)
+    ]
     if reps:
         part = lax.axis_index("rep")
         held[part] = pot * (1.0 / SCALE)
-        for d, partner in enumerate(twins):
-            copy = pltpu.make_async_remote_copy(
-                src_ref=held.at[part], dst_ref=held.at[part],
-                send_sem=rep_send.at[d], recv_sem=rep_recv.at[d],
-                device_id=partner, device_id_type=MESH,
-            )
-            copy.start()
-            seconds.append(copy)
-    for copy in copies:
+        rep_copies = [
+            remote(held.at[part], held.at[part], rep_send.at[d], rep_recv.at[d], partner)
+            for d, partner in enumerate(twins)
+        ]
+    for copy in seconds:
+        copy.wait_recv()
+    last = remote(full.at[core], full.at[core], twin_send.at[chips], twin_recv.at[chips], twin)
+    out[:, core] = full[core]
+    last.wait_recv()
+    out[:, 1 - core] = full[1 - core]
+    for copy in across + firsts + seconds + [last]:
         copy.wait_send()
-    for copy in seconds:
-        copy.wait()
-    out[...] = full[...]
     if reps:
+        for copy in rep_copies:
+            copy.wait()
         both[...] = held[...]
 
 
@@ -619,16 +630,17 @@
             return pot, None
         mine = lax.dynamic_slice_in_dim(pot, lax.axis_index("roll") * share, share, 0)
         return pot, lax.all_gather(mine, "rep") / SCALE
-    sums = sums.reshape(n, share, blk)
+    chips = n // 2
+    sums = sums.reshape(chips, 2, share, blk)
     dma = pltpu.SemaphoreType.DMA
     vmem = pl.BlockSpec(memory_space=pltpu.VMEM)
     both = (reps, share, blk)
     outs = [jax.ShapeDtypeStruct(sums.shape, sums.dtype)]
-    scratch = [pltpu.VMEM((n - 1, share, blk), jnp.float32), pltpu.VMEM((n, share, blk), jnp.float32)]
+    scratch = [pltpu.VMEM(shape + (share, blk), jnp.float32) for shape in ((chips,), (chips,), (chips - 1,), (2, chips))]
     if last:
         outs.append(jax.ShapeDtypeStruct(both, sums.dtype))
         scratch.append(pltpu.VMEM(both, jnp.float32))
-    scratch += [dma((n - 1,))] * 4
+    scratch += [dma((chips - 1,))] * 4 + [dma((chips + 1,))] * 2
     if last:
         scratch += [dma((reps - 1,))] * 2
     out = pl.pallas_call(

time: 102 us -> 102 us (level)
    pallas_call x2, Pallas kernels: 22 us -> 25.2 us  [column_potentials(): pl.pallas_call(functools.partial(column_kernel, n, reps if last else 0),...]
    pallas_call x1, Pallas kernels: 56.6 us -> 55.2 us  [gathered(): pl.pallas_call(functools.partial(gather_kernel, n, reps, slots), out_shap...]
where the time goes in v7:
time: 102 us
  Pallas kernels  99.5 us (98%)
  local copies, waits for them, and re-layouts  1.8 us (2%)
    pallas_call x1, Pallas kernels, gathered(): pl.pallas_call(functools.partial(gather_kernel, n, reps, slots), out_shap...  55.2 us
    pallas_call x2, Pallas kernels, column_potentials(): pl.pallas_call(functools.partial(column_kernel, n, reps if last else 0),...  25.2 us
    pallas_call x4, Pallas kernels, run_pass(): pl.pallas_call(functools.partial(pass_kernel, kind, fresh, stored), out_s...  11.4 us
    pallas_call x2, Pallas kernels, row_totals(): pl.pallas_call(functools.partial(row_kernel, reps, last), out_shape=[jax....  7.78 us

profile of v7, /device:TPU:0, one launch (start us, length us, event | category | flops | bytes accessed | tf_op | source)
XLA Modules:
  0.0 102.0 jit_solution(14997736545968857870)
XLA Ops:
  0.6 55.2 %gather_costs.1 = (f32[32768,128]{1,0:T(8,128)S(1)}, s32[8,384]{1,0:T(8,128)S(1)}) custom-call(bf16[2048,256]{1,0:T(8,128)(2,1)} %refs_0_.1, bf16[2048,256]{1,0:T(8,128)(2,1)} %refs_1_.1, bf16[256,256]{1,0:T(8,128)(2,1)} %refs_2_.1, s32[8,16]{1,0:T(8,128)} %bitcast.23, s32[1,16]{1,0:T(1,128)} %bitcast.25, s32[2,128]{1,0:T(2,128)} %bitcast.24), custom_call_target="tpu_custom_call" | custom-call | tf_op jit(solution)/shard_map/gather_costs/pallas_call | solution.py:544
  55.9 2.0 %pass_column.2 = f32[128,128]{1,0:T(8,128)S(1)} custom-call(s32[8,384]{1,0:T(8,128)S(1)} %get-tuple-element.9.lists_ref, f32[32768,128]{1,0:T(8,128)S(1)} %get-tuple-element.10.refs_0_), custom_call_target="tpu_custom_call" | custom-call | flops 16777216 | bytes 16777216 | tf_op jit(solution)/shard_map/pass_column/pallas_call | solution.py:138
  57.8 13.3 %column_exchange_0.1 = f32[8,2,8,128]{3,2,1,0:T(8,128)S(1)} custom-call(f32[8,2,8,128]{3,2,1,0:T(8,128)S(1)} %bitcast.15), custom_call_target="tpu_custom_call" | custom-call | tf_op jit(solution)/shard_map/column_exchange_0/pallas_call | solution.py:646
  71.1 2.8 %pass_row.1 = f32[1,32,128]{2,1,0:T(8,128)S(1)} custom-call(s32[8,384]{1,0:T(8,128)S(1)} %get-tuple-element.9.lists_ref, f32[32768,128]{1,0:T(8,128)S(1)} %get-tuple-element.10.refs_0_, f32[128,128]{1,0:T(8,128)S(1)} %bitcast.14), custom_call_target="tpu_custom_call" | custom-call | flops 16777216 | bytes 16777216 | tf_op jit(solution)/shard_map/pass_row/pallas_call | solution.py:138
  73.9 3.8 %row_exchange_0.1 = f32[2,16,128]{2,1,0:T(8,128)S(1)} custom-call(f32[1,2,16,128]{3,2,1,0:T(8,128)S(1)} %bitcast.18), custom_call_target="tpu_custom_call" | custom-call | tf_op jit(solution)/shard_map/row_exchange_0/pallas_call | solution.py:695
  77.7 2.9 %pass_column.3 = f32[128,128]{1,0:T(8,128)S(1)} custom-call(s32[8,384]{1,0:T(8,128)S(1)} %get-tuple-element.9.lists_ref, f32[32768,128]{1,0:T(8,128)S(1)} %get-tuple-element.10.refs_0_, f32[32,128]{1,0:T(8,128)S(1)} %bitcast.19), custom_call_target="tpu_custom_call" | custom-call | flops 16777216 | bytes 16777216 | tf_op jit(solution)/shard_map/pass_column/pallas_call | solution.py:138
  80.6 11.9 %column_exchange_1.1 = (f32[8,2,8,128]{3,2,1,0:T(8,128)S(1)}, f32[2,8,128]{2,1,0:T(8,128)S(1)}) custom-call(f32[8,2,8,128]{3,2,1,0:T(8,128)S(1)} %bitcast.13), custom_call_target="tpu_custom_call" | custom-call | tf_op jit(solution)/shard_map/column_exchange_1/pallas_call | solution.py:646
  92.5 3.8 %pass_final.1 = f32[2,32,128]{2,1,0:T(8,128)S(1)} custom-call(s32[8,384]{1,0:T(8,128)S(1)} %get-tuple-element.9.lists_ref, f32[32768,128]{1,0:T(8,128)S(1)} %get-tuple-element.10.refs_0_, f32[128,128]{1,0:T(8,128)S(1)} %bitcast.17), custom_call_target="tpu_custom_call" | custom-call | flops 16777216 | bytes 16777216 | tf_op jit(solution)/shard_map/pass_final/pallas_call | solution.py:138
  96.3 4.0 %row_exchange_1.1 = (f32[16,128]{1,0:T(8,128)S(1)}, f32[16,128]{1,0:T(8,128)S(1)}) custom-call(f32[2,2,16,128]{3,2,1,0:T(8,128)S(1)} %bitcast.16), custom_call_target="tpu_custom_call" | custom-call | tf_op jit(solution)/shard_map/row_exchange_1/pallas_call | solution.py:695
  100.2 0.6 copy.12
  100.8 0.6 copy.13
  101.4 0.6 copy.14
